TPU v7x, 128 devices: a whole 4x4x4 slice. The times are simulated.
128 devices in a mesh: ctx: 8 (over x, core), head: 16 (over z, y).
Axes of the slice: x: 4, y: 4, z: 4, core: 2. Of those that a mesh axis runs over, the one named last changes fastest.
Arguments:
- inputs: bfloat16 [512, 16384], P('head', 'ctx'), may hold values from -6 to 6
- gate: bfloat16 [512, 16384], P('head', 'ctx'), may hold values from -6 to 6
- filter_taps: float32 [512, 16384], P('head', 'ctx'), may hold values from -0.078125 to 0.078125
- skip: float32 [512], P('head'), may hold values from 0.5 to 1.5
- w_out: bfloat16 [512, 512], P('head'), may hold values from -0.25 to 0.25
- far_pairs: int32 [16, 4], P('ctx'), may hold values from -1 to 13, as said below
Outputs:
- projected: float32 [512, 16384], P('head', 'ctx')
Inputs may be any that keep to these rules, and one draw needn't show every extreme that they name: `far_pairs`: row i lists i - 2 first when i >= 2, else -1; its other entries are distinct blocks below i - 2, or -1 where fewer exist.
All inputs are finite; a program needn't handle non-finite values.
Results may differ from a plain program's by a relative error of at most 0.0029.
Values may be sent and summed in bfloat16 or wider, within the bound.
A program may use at most 128 MiB of HBM per device.

v0:
```python
import jax
import jax.numpy as jnp
from jax import lax
from jax.experimental import pallas as pl
from jax.experimental.pallas import tpu as pltpu
from jax.sharding import PartitionSpec as P

F32 = jnp.float32
BF16 = jnp.bfloat16
LANES = 128
BLOCKS = 16
SUBS = 8
PIECES = BLOCKS * SUBS
NC = 8
NH = 16
CH = 32
MINE = CH // NC
ROWS = 16
PER = 3 * ROWS
WIN = 2
MESH = pl.DeviceIdType.MESH


def greet(me_c, me_h):
    barrier = pltpu.get_barrier_semaphore()
    for k in range(1, NC):
        pl.semaphore_signal(
            barrier, inc=1, device_id={"ctx": lax.rem(me_c + k, NC)}, device_id_type=MESH
        )
    for k in range(1, NH):
        pl.semaphore_signal(
            barrier, inc=1, device_id={"head": lax.rem(me_h + k, NH)}, device_id_type=MESH
        )
    pl.semaphore_wait(barrier, NC - 1 + NH - 1)


def spread_kernel(
    x_ref, g_ref, h_ref, w_ref, far_ref, got, far_got, w_got,
    stage, packed, far_mine, send_sem, recv_sem, far_send, far_recv, w_send, w_recv, own_sem,
):
    me_c, me_h = lax.axis_index("ctx"), lax.axis_index("head")
    row = lax.broadcasted_iota(jnp.int32, (8, LANES), 0)
    table = jnp.full((8, LANES), -1, jnp.int32)
    for r in range(2):
        for k in range(4):
            table = jnp.where(row == 4 * r + k, far_ref[r, k], table)
    far_mine[...] = table
    greet(me_c, me_h)

    def w_copy(k):
        peer = lax.rem(me_h + k, NH)
        return pltpu.make_async_remote_copy(
            src_ref=w_ref, dst_ref=w_got.at[me_h], send_sem=w_send.at[k], recv_sem=w_recv.at[k],
            device_id={"head": peer}, device_id_type=MESH,
        )

    def far_copy(k):
        peer = lax.rem(me_c + k, NC)
        return pltpu.make_async_remote_copy(
            src_ref=far_mine, dst_ref=far_got.at[me_c], send_sem=far_send.at[k], recv_sem=far_recv.at[k],
            device_id={"ctx": peer}, device_id_type=MESH,
        )

    def copy(k):
        peer = lax.rem(me_c + k, NC)
        return pltpu.make_async_remote_copy(
            src_ref=packed.at[peer], dst_ref=got.at[me_c], send_sem=send_sem.at[k], recv_sem=recv_sem.at[k],
            device_id={"ctx": peer}, device_id_type=MESH,
        )

    for k in range(1, NC):
        far_copy(k).start()
    for a, ref in enumerate((h_ref, x_ref, g_ref)):
        for s in range(ROWS):
            stage[a, pl.ds(s, CH, stride=ROWS), :] = ref[:, LANES * s : LANES * (s + 1)].astype(F32)
        for c in range(NC):
            for m in range(MINE):
                ch = MINE * c + m
                packed[c, PER * m + ROWS * a : PER * m + ROWS * (a + 1), :] = stage[
                    a, ROWS * ch : ROWS * (ch + 1), :
                ].astype(BF16)
    for k in range(1, NC):
        copy(k).start()
    for k in range(1, NH):
        w_copy(k).start()
    own = pltpu.make_async_copy(packed.at[me_c], got.at[me_c], own_sem.at[0])
    own_far = pltpu.make_async_copy(far_mine, far_got.at[me_c], own_sem.at[1])
    own_w = pltpu.make_async_copy(w_ref, w_got.at[me_h], own_sem.at[2])
    for c in (own, own_far, own_w):
        c.start()
    for c in (own, own_far, own_w):
        c.wait()
    for k in range(1, NC):
        far_copy(k).wait()
        copy(k).wait()
    for k in range(1, NH):
        w_copy(k).wait()


def shifted_taps(taps, big):
    lane = lax.broadcasted_iota(jnp.int32, (16, LANES), 1)
    keep = lane >= lax.broadcasted_iota(jnp.int32, (16, LANES), 0)
    big[0] = jnp.zeros((LANES, LANES), BF16)

    def step(p, carry):
        before, edges = carry
        row = jnp.broadcast_to(taps[pl.ds(p, 1), :], (16, LANES))
        turned = pltpu.roll(row, 0, 1, stride=1, stride_axis=0)
        edge = jnp.where(keep, turned, before).astype(BF16)
        big[p + 1, 0:16, :] = edge
        rolled = []
        for k in range(1, 8):
            r = pltpu.roll(edge, 16 * k, 1)
            big[p + 1, 16 * k : 16 * k + 16, :] = jnp.where(lane >= 16 * k, r, edges[k - 1])
            rolled.append(r)
        return turned, tuple(rolled)

    zero = jnp.zeros((16, LANES), F32)
    lax.fori_loop(0, PIECES, step, (zero, (zero.astype(BF16),) * 7), unroll=16)


def conv_kernel(got, far_got, skip_ref, out, taps, padded, wide, mixed, masks, source, big):
    me_c = lax.axis_index("ctx")
    for d in range(BLOCKS):
        block = lax.broadcasted_iota(jnp.int32, (BLOCKS, LANES), 0)
        mask = jnp.full((BLOCKS, LANES), 1.0 if d < WIN else 0.0, F32)
        if d >= WIN:
            for k in range(4):
                mask = jnp.where(far_got[pl.ds(k, BLOCKS, stride=4), :] == block - d, 1.0, mask)
        masks[d] = mask
    for b in range(SUBS):
        padded[b, 0:BLOCKS, :] = jnp.zeros((BLOCKS, LANES), F32)
    for b in range(4):
        source[BLOCKS, b] = jnp.zeros((BLOCKS, 256), BF16)

    def channel(m, _):
        for c in range(NC):
            base = pl.multiple_of(m * PER, 16)
            taps[ROWS * c : ROWS * (c + 1), :] = got[c, pl.ds(base, 16), :].astype(F32)
            wide[ROWS * c : ROWS * (c + 1), :] = got[c, pl.ds(base + 16, 16), :].astype(F32)
        for b in range(SUBS):
            padded[b, BLOCKS : 2 * BLOCKS, :] = wide[pl.ds(b, BLOCKS, stride=SUBS), :]
        for d in range(BLOCKS):
            mask = masks[d]
            for b in range(SUBS):
                lo = LANES * (b % 2)
                source[d, b // 2, :, lo : lo + LANES] = (
                    padded[b, BLOCKS - d : 2 * BLOCKS - d, :] * mask
                ).astype(BF16)
        shifted_taps(taps, big)

        def group(q4, acc):
            for u in range(4):
                rows = []
                for a in range(4):
                    b = (a - u) % 4
                    rows.append(source[q4 + (u - a + b) // 4, b])
                q = 4 * q4 + u
                here, after, before = big[2 * q + 1], big[2 * q + 2], big[2 * q]
                right = jnp.concatenate(
                    [
                        jnp.concatenate([here, after], axis=1),
                        jnp.concatenate([before, here], axis=1),
                    ],
                    axis=0,
                )
                acc = acc + jnp.dot(
                    jnp.concatenate(rows, axis=0), right, preferred_element_type=F32
                )
            return acc

        acc = lax.fori_loop(0, BLOCKS, group, jnp.zeros((64, 256), F32), unroll=2)
        for c in range(NC):
            base = pl.multiple_of(m * PER, 16)
            wide[ROWS * c : ROWS * (c + 1), :] = got[c, pl.ds(base + 32, 16), :].astype(F32)
        skip = skip_ref[MINE * me_c + m]
        for b in range(SUBS):
            a, lo = b // 2, LANES * (b % 2)
            y = acc[16 * a : 16 * a + 16, lo : lo + LANES] + skip * padded[b, BLOCKS : 2 * BLOCKS, :]
            mixed[pl.ds(b, BLOCKS, stride=SUBS), :] = wide[pl.ds(b, BLOCKS, stride=SUBS), :] * y
        for c in range(NC):
            out[c, pl.ds(pl.multiple_of(m * ROWS, 16), ROWS), :] = mixed[
                ROWS * c : ROWS * (c + 1), :
            ].astype(BF16)
        return 0

    lax.fori_loop(0, MINE, channel, 0)


def project_kernel(
    mixed, w, out, got, stage, sliced, part, result,
    m_send, m_recv, t_send, t_recv, o_send, o_recv, own_sem,
):
    me_c, me_h = lax.axis_index("ctx"), lax.axis_index("head")
    greet(me_c, me_h)

    def m_copy(k):
        peer = lax.rem(me_c + k, NC)
        return pltpu.make_async_remote_copy(
            src_ref=mixed.at[peer], dst_ref=got.at[me_c], send_sem=m_send.at[k], recv_sem=m_recv.at[k],
            device_id={"ctx": peer}, device_id_type=MESH,
        )

    def t_copy(k):
        peer = lax.rem(me_h + k, NH)
        return pltpu.make_async_remote_copy(
            src_ref=sliced.at[peer], dst_ref=part.at[me_h], send_sem=t_send.at[k], recv_sem=t_recv.at[k],
            device_id={"head": peer}, device_id_type=MESH,
        )

    def o_copy(k):
        peer = lax.rem(me_h + k, NH)
        return pltpu.make_async_remote_copy(
            src_ref=result.at[peer],
            dst_ref=out.at[:, pl.ds(pl.multiple_of(me_h * LANES, LANES), LANES)],
            send_sem=o_send.at[k], recv_sem=o_recv.at[k],
            device_id={"head": peer}, device_id_type=MESH,
        )

    for k in range(1, NC):
        m_copy(k).start()
    own = pltpu.make_async_copy(mixed.at[me_c], got.at[me_c], own_sem.at[0])
    own.start()
    own.wait()
    for k in range(1, NC):
        m_copy(k).wait()
    for c in range(NC):
        stage[64 * c : 64 * c + 64, :] = got[c].astype(F32)
    for t in range(NH):
        sliced[t] = stage[pl.ds(t, CH, stride=NH), :].astype(BF16)
    for k in range(1, NH):
        t_copy(k).start()
    own = pltpu.make_async_copy(sliced.at[me_h], part.at[me_h], own_sem.at[1])
    own.start()
    own.wait()
    for k in range(1, NH):
        t_copy(k).wait()
    total = lax.dot_general(
        w[...].reshape(NH * CH, NH * CH), part[...].reshape(NH * CH, LANES),
        (((0,), (0,)), ((), ())), preferred_element_type=F32,
    )
    for t in range(NH):
        result[t] = total[CH * t : CH * (t + 1), :]
    for k in range(1, NH):
        o_copy(k).start()
    own = pltpu.make_async_copy(
        result.at[me_h], out.at[:, pl.ds(pl.multiple_of(me_h * LANES, LANES), LANES)], own_sem.at[2]
    )
    own.start()
    own.wait()
    for k in range(1, NH):
        o_copy(k).wait()


def local(inputs, gate, filter_taps, skip, w_out, far_pairs):
    vmem = pl.BlockSpec(memory_space=pltpu.VMEM)
    smem = pl.BlockSpec(memory_space=pltpu.SMEM)
    dma = pltpu.SemaphoreType.DMA
    got, far_got, w_all = pl.pallas_call(
        spread_kernel,
        out_shape=[
            jax.ShapeDtypeStruct((NC, MINE * PER, LANES), BF16),
            jax.ShapeDtypeStruct((NC, 8, LANES), jnp.int32),
            jax.ShapeDtypeStruct((NH, CH, NH * CH), BF16),
        ],
        in_specs=[vmem] * 4 + [smem],
        out_specs=[vmem] * 3,
        scratch_shapes=[
            pltpu.VMEM((3, CH * ROWS, LANES), F32),
            pltpu.VMEM((NC, MINE * PER, LANES), BF16),
            pltpu.VMEM((8, LANES), jnp.int32),
            dma((NC,)), dma((NC,)), dma((NC,)), dma((NC,)), dma((NH,)), dma((NH,)), dma((3,)),
        ],
        compiler_params=pltpu.CompilerParams(
            collective_id=0, has_side_effects=True, vmem_limit_bytes=40 << 20
        ),
    )(inputs, gate, filter_taps, w_out, far_pairs)
    mixed = pl.pallas_call(
        conv_kernel,
        out_shape=jax.ShapeDtypeStruct((NC, MINE * ROWS, LANES), BF16),
        in_specs=[vmem, vmem, smem],
        out_specs=vmem,
        scratch_shapes=[
            pltpu.VMEM((PIECES, LANES), F32),
            pltpu.VMEM((SUBS, 2 * BLOCKS, LANES), F32),
            pltpu.VMEM((PIECES, LANES), F32),
            pltpu.VMEM((PIECES, LANES), F32),
            pltpu.VMEM((BLOCKS, BLOCKS, LANES), F32),
            pltpu.VMEM((BLOCKS + 1, 4, BLOCKS, 256), BF16),
            pltpu.VMEM((PIECES + 1, LANES, LANES), BF16),
        ],
        compiler_params=pltpu.CompilerParams(vmem_limit_bytes=40 << 20),
    )(got, far_got.reshape(NC * 8, LANES), skip)
    return pl.pallas_call(
        project_kernel,
        out_shape=jax.ShapeDtypeStruct((CH, NH * LANES), F32),
        in_specs=[vmem, vmem],
        out_specs=vmem,
        scratch_shapes=[
            pltpu.VMEM((NC, MINE * ROWS, LANES), BF16),
            pltpu.VMEM((CH * ROWS, LANES), F32),
            pltpu.VMEM((NH, CH, LANES), BF16),
            pltpu.VMEM((NH, CH, LANES), BF16),
            pltpu.VMEM((NH, CH, LANES), F32),
            dma((NC,)), dma((NC,)), dma((NH,)), dma((NH,)), dma((NH,)), dma((NH,)), dma((3,)),
        ],
        compiler_params=pltpu.CompilerParams(
            collective_id=1, has_side_effects=True, vmem_limit_bytes=40 << 20
        ),
    )(mixed, w_all)


def solution(mesh):
    in_specs = (
        P("head", "ctx"),
        P("head", "ctx"),
        P("head", "ctx"),
        P("head"),
        P("head", None),
        P("ctx", None),
    )
    out_specs = P("head", "ctx")
    return jax.shard_map(local, mesh=mesh, in_specs=in_specs, out_specs=out_specs, check_vma=False)
```

profile of v0, /device:TPU:0, one launch (start us, length us, event | category | flops | bytes accessed | tf_op | source)
XLA Modules:
  0.0 63.1 jit_solution(15232106067949330180)
XLA Ops:
  0.0 0.0 copy-start
  0.0 0.9 %copy-done = f32[32,2048]{1,0:T(8,128)S(1)} copy-done((f32[32,2048]{1,0:T(8,128)S(1)}, f32[32,2048]{1,0:T(8,128)}, u32[]{:S(2)}) %copy-start) | copy-done | bytes 262168
  1.0 0.0 copy-start.1
  1.0 0.9 %copy-done.1 = bf16[32,2048]{1,0:T(8,128)(2,1)S(1)} copy-done((bf16[32,2048]{1,0:T(8,128)(2,1)S(1)}, bf16[32,2048]{1,0:T(8,128)(2,1)}, u32[]{:S(2)}) %copy-start.1) | copy-done | bytes 131096
  1.9 0.0 copy-start.2
  1.9 0.9 %copy-done.2 = bf16[32,2048]{1,0:T(8,128)(2,1)S(1)} copy-done((bf16[32,2048]{1,0:T(8,128)(2,1)S(1)}, bf16[32,2048]{1,0:T(8,128)(2,1)}, u32[]{:S(2)}) %copy-start.2) | copy-done | bytes 131096
  2.8 0.0 copy-start.3
  2.8 0.8 %copy-done.3 = bf16[32,512]{1,0:T(8,128)(2,1)S(1)} copy-done((bf16[32,512]{1,0:T(8,128)(2,1)S(1)}, bf16[32,512]{1,0:T(8,128)(2,1)}, u32[]{:S(2)}) %copy-start.3) | copy-done | bytes 32792
  3.5 0.0 copy-start.4
  3.5 0.7 %copy-done.4 = s32[2,4]{1,0:T(2,128)S(1)} copy-done((s32[2,4]{1,0:T(2,128)S(1)}, s32[2,4]{1,0:T(2,128)}, u32[]{:S(2)}) %copy-start.4) | copy-done | bytes 56
  4.2 16.1 %shard_map.64 = (bf16[8,192,128]{2,1,0:T(8,128)(2,1)S(1)}, s32[8,8,128]{2,1,0:T(8,128)S(1)}, bf16[16,32,512]{2,1,0:T(8,128)(2,1)S(1)}) custom-call(bf16[32,2048]{1,0:T(8,128)(2,1)S(1)} %copy-done.1, bf16[32,2048]{1,0:T(8,128)(2,1)S(1)} %copy-done.2, f32[32,2048]{1,0:T(8,128)S(1)} %copy-done, bf16[32,512]{1,0:T(8,128)(2,1)S(1)} %copy-done.3, s32[2,4]{1,0:T(2,128)S(1)} %copy-done.4), custom_call_target="tpu_custom_call" | custom-call | tf_op jit(solution)/shard_map/pallas_call | solution.py:259
  20.3 0.0 copy-start.5
  20.3 0.6 %copy-done.5 = f32[32]{0:T(128)S(1)} copy-done((f32[32]{0:T(128)S(1)}, f32[32]{0:T(128)}, u32[]{:S(2)}) %copy-start.5) | copy-done | bytes 152
  21.0 20.4 %shard_map.65.mixed = bf16[8,64,128]{2,1,0:T(8,128)(2,1)S(1)} custom-call(bf16[8,192,128]{2,1,0:T(8,128)(2,1)S(1)} %get-tuple-element.8.got, s32[64,128]{1,0:T(8,128)S(1)} %bitcast.1, f32[32]{0:T(128)S(1)} %copy-done.5), custom_call_target="tpu_custom_call" | custom-call | tf_op jit(solution)/shard_map/pallas_call | solution.py:278
  41.4 21.0 %shard_map.66 = f32[32,2048]{1,0:T(8,128)S(1)} custom-call(bf16[8,64,128]{2,1,0:T(8,128)(2,1)S(1)} %shard_map.65.mixed, bf16[16,32,512]{2,1,0:T(8,128)(2,1)S(1)} %get-tuple-element.10.w), custom_call_target="tpu_custom_call" | custom-call | tf_op jit(solution)/shard_map/pallas_call | solution.py:294
  62.4 0.7 %copy.8 = f32[32,2048]{1,0:T(8,128)} copy(f32[32,2048]{1,0:T(8,128)S(1)} %shard_map.66) | data formatting | bytes 524288
Async XLA Ops:
  0.0 0.9 %copy-start = (f32[32,2048]{1,0:T(8,128)S(1)}, f32[32,2048]{1,0:T(8,128)}, u32[]{:S(2)}) copy-start(f32[32,2048]{1,0:T(8,128)} %h_ref.1) | copy-start | bytes 786436
  1.0 0.9 %copy-start.1 = (bf16[32,2048]{1,0:T(8,128)(2,1)S(1)}, bf16[32,2048]{1,0:T(8,128)(2,1)}, u32[]{:S(2)}) copy-start(bf16[32,2048]{1,0:T(8,128)(2,1)} %x_ref.1) | copy-start | bytes 393220
  1.9 0.9 %copy-start.2 = (bf16[32,2048]{1,0:T(8,128)(2,1)S(1)}, bf16[32,2048]{1,0:T(8,128)(2,1)}, u32[]{:S(2)}) copy-start(bf16[32,2048]{1,0:T(8,128)(2,1)} %g_ref.1) | copy-start | bytes 393220
  2.8 0.8 %copy-start.3 = (bf16[32,512]{1,0:T(8,128)(2,1)S(1)}, bf16[32,512]{1,0:T(8,128)(2,1)}, u32[]{:S(2)}) copy-start(bf16[32,512]{1,0:T(8,128)(2,1)} %w_ref.1) | copy-start | bytes 98308
  3.5 0.7 %copy-start.4 = (s32[2,4]{1,0:T(2,128)S(1)}, s32[2,4]{1,0:T(2,128)}, u32[]{:S(2)}) copy-start(s32[2,4]{1,0:T(2,128)} %far_ref.1) | copy-start | bytes 100
  20.3 0.7 %copy-start.5 = (f32[32]{0:T(128)S(1)}, f32[32]{0:T(128)}, u32[]{:S(2)}) copy-start(f32[32]{0:T(128)} %skip_ref.1) | copy-start | bytes 388
where the time goes:
time: 63.4 us; the launch traced here: 63.1 us
  Pallas kernels  57.6 us (91%)
  local copies, waits for them, and re-layouts  5.55 us (9%)
    pallas_call x1, Pallas kernels, local(): pl.pallas_call(project_kernel, out_shape=jax.ShapeDtypeStruct((CH, NH * L...  21 us
    pallas_call x1, Pallas kernels, local(): pl.pallas_call(conv_kernel, out_shape=jax.ShapeDtypeStruct((NC, MINE * RO...  20.4 us
    pallas_call x1, Pallas kernels, local(): pl.pallas_call(spread_kernel, out_shape=[jax.ShapeDtypeStruct((NC, MINE *...  16.1 us
    unnamed x13, local copies, waits for them, and re-layouts  5.55 us

commit v1 on v0

v1 whole, which is shorter than its diff:
```python
import jax
import jax.numpy as jnp
from jax import lax
from jax.experimental import pallas as pl
from jax.experimental.pallas import tpu as pltpu
from jax.sharding import PartitionSpec as P

F32 = jnp.float32
BF16 = jnp.bfloat16
LANES = 128
BLOCKS = 16
SUBS = 8
PIECES = BLOCKS * SUBS
NC = 8
NH = 16
CH = 32
MINE = CH // NC
ROWS = 16
PER = 3 * ROWS
WIN = 2
MESH = pl.DeviceIdType.MESH


def greet(me_c, me_h):
    barrier = pltpu.get_barrier_semaphore()
    for k in range(1, NC):
        pl.semaphore_signal(
            barrier, inc=1, device_id={"ctx": lax.rem(me_c + k, NC)}, device_id_type=MESH
        )
    for k in range(1, NH):
        pl.semaphore_signal(
            barrier, inc=1, device_id={"head": lax.rem(me_h + k, NH)}, device_id_type=MESH
        )


def shifted_taps(taps, big):
    lane = lax.broadcasted_iota(jnp.int32, (16, LANES), 1)
    keep = lane >= lax.broadcasted_iota(jnp.int32, (16, LANES), 0)
    big[0] = jnp.zeros((LANES, LANES), BF16)

    def step(p, carry):
        before, edges = carry
        row = jnp.broadcast_to(taps[pl.ds(p, 1), :], (16, LANES))
        turned = pltpu.roll(row, 0, 1, stride=1, stride_axis=0)
        edge = jnp.where(keep, turned, before).astype(BF16)
        big[p + 1, 0:16, :] = edge
        rolled = []
        for k in range(1, 8):
            r = pltpu.roll(edge, 16 * k, 1)
            big[p + 1, 16 * k : 16 * k + 16, :] = jnp.where(lane >= 16 * k, r, edges[k - 1])
            rolled.append(r)
        return turned, tuple(rolled)

    zero = jnp.zeros((16, LANES), F32)
    lax.fori_loop(0, PIECES, step, (zero, (zero.astype(BF16),) * 7), unroll=16)


def fill(me_c, m, got, lo, wide):
    for c in range(NC):
        base = pl.multiple_of(m * PER + lo, 16)
        wide[ROWS * c : ROWS * (c + 1), :] = got[c, pl.ds(base, ROWS), :].astype(F32)


def kernel(
    x_hbm, g_hbm, h_hbm, w_hbm, far_hbm, skip_hbm, out,
    x_in, g_in, h_in, w_in, far_in, skip_in,
    stage, packed, got, far_mine, far_got, w_got,
    taps, padded, wide, mixed, masks, source, big,
    ready, back, regroup, sliced, part, result,
    load_sem, own_sem, in_send, in_recv, far_send, far_recv, w_send, w_recv,
    m_send, m_recv, t_send, t_recv, o_send, o_recv,
):
    me_c, me_h = lax.axis_index("ctx"), lax.axis_index("head")

    def remote(src, dst, send, recv, axis, k):
        me, n = (me_c, NC) if axis == "ctx" else (me_h, NH)
        return pltpu.make_async_remote_copy(
            src_ref=src, dst_ref=dst, send_sem=send, recv_sem=recv,
            device_id={axis: lax.rem(me + k, n)}, device_id_type=MESH,
        )

    def far_copy(k):
        return remote(far_mine, far_got.at[me_c], far_send.at[k], far_recv.at[k], "ctx", k)

    def w_copy(k):
        return remote(w_in, w_got.at[me_h], w_send.at[k], w_recv.at[k], "head", k)

    def in_copy(m, k):
        rows = pl.ds(pl.multiple_of(m * PER, 16), PER)
        peer = lax.rem(me_c + k, NC)
        return remote(
            packed.at[peer, rows], got.at[me_c, rows], in_send.at[m, k], in_recv.at[m, k], "ctx", k
        )

    def m_copy(m, k):
        rows = pl.ds(pl.multiple_of(m * ROWS, 16), ROWS)
        peer = lax.rem(me_c + k, NC)
        return remote(
            ready.at[peer, rows], back.at[me_c, rows], m_send.at[m, k], m_recv.at[m, k], "ctx", k
        )

    def t_copy(k):
        peer = lax.rem(me_h + k, NH)
        return remote(sliced.at[peer], part.at[me_h], t_send.at[k], t_recv.at[k], "head", k)

    columns = pl.ds(pl.multiple_of(me_h * LANES, LANES), LANES)

    def o_copy(k):
        peer = lax.rem(me_h + k, NH)
        return remote(result.at[peer], out.at[:, columns], o_send.at[k], o_recv.at[k], "head", k)

    loads = [
        pltpu.make_async_copy(a, b, load_sem.at[i])
        for i, (a, b) in enumerate(
            (
                (h_hbm, h_in), (x_hbm, x_in), (g_hbm, g_in), (far_hbm, far_in),
                (skip_hbm, skip_in), (w_hbm, w_in),
            )
        )
    ]
    for copy in loads:
        copy.start()
    greet(me_c, me_h)
    for copy in loads:
        copy.wait()
    row = lax.broadcasted_iota(jnp.int32, (8, LANES), 0)
    table = jnp.full((8, LANES), -1, jnp.int32)
    for r in range(2):
        for k in range(4):
            table = jnp.where(row == 4 * r + k, far_in[r, k], table)
    far_mine[...] = table
    for a, ref in enumerate((h_in, x_in, g_in)):
        for s in range(ROWS):
            stage[a, pl.ds(s, CH, stride=ROWS), :] = ref[:, LANES * s : LANES * (s + 1)].astype(F32)
        for c in range(NC):
            for m in range(MINE):
                ch = MINE * c + m
                packed[c, PER * m + ROWS * a : PER * m + ROWS * (a + 1), :] = stage[
                    a, ROWS * ch : ROWS * (ch + 1), :
                ].astype(BF16)
    pl.semaphore_wait(pltpu.get_barrier_semaphore(), NC - 1 + NH - 1)

    for k in range(1, NC):
        far_copy(k).start()
    for m in range(MINE):
        for k in range(1, NC):
            in_copy(m, k).start()
    for k in range(1, NH):
        w_copy(k).start()
    own = [
        pltpu.make_async_copy(a, b, own_sem.at[i])
        for i, (a, b) in enumerate(
            (
                (far_mine, far_got.at[me_c]), (packed.at[me_c], got.at[me_c]), (w_in, w_got.at[me_h]),
            )
        )
    ]
    for copy in own:
        copy.start()
    for copy in own:
        copy.wait()
    for b in range(SUBS):
        padded[b, 0:BLOCKS, :] = jnp.zeros((BLOCKS, LANES), F32)
    for b in range(4):
        source[BLOCKS, b] = jnp.zeros((BLOCKS, 256), BF16)
    for k in range(1, NC):
        far_copy(k).wait()
    for c in range(NC):
        regroup[8 * c : 8 * c + 8, :] = far_got[c]
    for d in range(BLOCKS):
        block = lax.broadcasted_iota(jnp.int32, (BLOCKS, LANES), 0)
        mask = jnp.full((BLOCKS, LANES), 1.0 if d < WIN else 0.0, F32)
        if d >= WIN:
            for k in range(4):
                mask = jnp.where(regroup[pl.ds(k, BLOCKS, stride=4), :] == block - d, 1.0, mask)
        masks[d] = mask

    def channel(m, _):
        for k in range(1, NC):
            in_copy(m, k).wait()
        fill(me_c, m, got, 0, taps)
        fill(me_c, m, got, ROWS, wide)
        for b in range(SUBS):
            padded[b, BLOCKS : 2 * BLOCKS, :] = wide[pl.ds(b, BLOCKS, stride=SUBS), :]
        for d in range(BLOCKS):
            mask = masks[d]
            for b in range(SUBS):
                lo = LANES * (b % 2)
                source[d, b // 2, :, lo : lo + LANES] = (
                    padded[b, BLOCKS - d : 2 * BLOCKS - d, :] * mask
                ).astype(BF16)
        shifted_taps(taps, big)

        def group(q4, acc):
            for u in range(4):
                rows = []
                for a in range(4):
                    b = (a - u) % 4
                    rows.append(source[q4 + (u - a + b) // 4, b])
                q = 4 * q4 + u
                here, after, before = big[2 * q + 1], big[2 * q + 2], big[2 * q]
                right = jnp.concatenate(
                    [
                        jnp.concatenate([here, after], axis=1),
                        jnp.concatenate([before, here], axis=1),
                    ],
                    axis=0,
                )
                acc = acc + jnp.dot(
                    jnp.concatenate(rows, axis=0), right, preferred_element_type=F32
                )
            return acc

        acc = lax.fori_loop(0, BLOCKS, group, jnp.zeros((64, 256), F32), unroll=2)
        fill(me_c, m, got, 2 * ROWS, wide)
        skip = skip_in[MINE * me_c + m]
        for b in range(SUBS):
            a, lo = b // 2, LANES * (b % 2)
            y = acc[16 * a : 16 * a + 16, lo : lo + LANES] + skip * padded[b, BLOCKS : 2 * BLOCKS, :]
            mixed[pl.ds(b, BLOCKS, stride=SUBS), :] = wide[pl.ds(b, BLOCKS, stride=SUBS), :] * y
        for c in range(NC):
            ready[c, pl.ds(pl.multiple_of(m * ROWS, 16), ROWS), :] = mixed[
                ROWS * c : ROWS * (c + 1), :
            ].astype(BF16)
        for k in range(1, NC):
            m_copy(m, k).start()
        return 0

    lax.fori_loop(0, MINE, channel, 0)
    copy = pltpu.make_async_copy(ready.at[me_c], back.at[me_c], own_sem.at[3])
    copy.start()
    copy.wait()
    for m in range(MINE):
        for k in range(1, NC):
            m_copy(m, k).wait()
    for c in range(NC):
        stage[0, 64 * c : 64 * c + 64, :] = back[c].astype(F32)
    for t in range(NH):
        sliced[t] = stage[0, pl.ds(t, CH, stride=NH), :].astype(BF16)
    for k in range(1, NH):
        t_copy(k).start()
    copy = pltpu.make_async_copy(sliced.at[me_h], part.at[me_h], own_sem.at[4])
    copy.start()
    copy.wait()
    for k in range(1, NH):
        w_copy(k).wait()
    for k in range(1, NH):
        t_copy(k).wait()
    total = lax.dot_general(
        w_got[...].reshape(NH * CH, NH * CH), part[...].reshape(NH * CH, LANES),
        (((0,), (0,)), ((), ())), preferred_element_type=F32,
    )
    for t in range(NH):
        result[t] = total[CH * t : CH * (t + 1), :]
    for k in range(1, NH):
        o_copy(k).start()
    copy = pltpu.make_async_copy(result.at[me_h], out.at[:, columns], own_sem.at[5])
    copy.start()
    copy.wait()
    for k in range(1, NH):
        o_copy(k).wait()


def local(inputs, gate, filter_taps, skip, w_out, far_pairs):
    hbm = pl.BlockSpec(memory_space=pltpu.HBM)
    dma = pltpu.SemaphoreType.DMA
    vmem = pltpu.VMEM
    return pl.pallas_call(
        kernel,
        out_shape=jax.ShapeDtypeStruct((CH, NH * LANES), F32),
        in_specs=[hbm] * 6,
        out_specs=hbm,
        scratch_shapes=[
            vmem(inputs.shape, BF16), vmem(gate.shape, BF16), vmem(filter_taps.shape, F32),
            vmem(w_out.shape, BF16), pltpu.SMEM(far_pairs.shape, jnp.int32), pltpu.SMEM(skip.shape, F32),
            vmem((3, CH * ROWS, LANES), F32),
            vmem((NC, MINE * PER, LANES), BF16),
            vmem((NC, MINE * PER, LANES), BF16),
            vmem((8, LANES), jnp.int32),
            vmem((NC, 8, LANES), jnp.int32),
            vmem((NH, CH, NH * CH), BF16),
            vmem((PIECES, LANES), F32),
            vmem((SUBS, 2 * BLOCKS, LANES), F32),
            vmem((PIECES, LANES), F32),
            vmem((PIECES, LANES), F32),
            vmem((BLOCKS, BLOCKS, LANES), F32),
            vmem((BLOCKS + 1, 4, BLOCKS, 256), BF16),
            vmem((PIECES + 1, LANES, LANES), BF16),
            vmem((NC, MINE * ROWS, LANES), BF16),
            vmem((NC, MINE * ROWS, LANES), BF16),
            vmem((NC * 8, LANES), jnp.int32),
            vmem((NH, CH, LANES), BF16),
            vmem((NH, CH, LANES), BF16),
            vmem((NH, CH, LANES), F32),
            dma((6,)), dma((6,)), dma((MINE, NC)), dma((MINE, NC)), dma((NC,)), dma((NC,)),
            dma((NH,)), dma((NH,)), dma((MINE, NC)), dma((MINE, NC)),
            dma((NH,)), dma((NH,)), dma((NH,)), dma((NH,)),
        ],
        compiler_params=pltpu.CompilerParams(
            collective_id=0, has_side_effects=True, vmem_limit_bytes=40 << 20
        ),
    )(inputs, gate, filter_taps, w_out, far_pairs, skip)


def solution(mesh):
    in_specs = (
        P("head", "ctx"),
        P("head", "ctx"),
        P("head", "ctx"),
        P("head"),
        P("head", None),
        P("ctx", None),
    )
    out_specs = P("head", "ctx")
    return jax.shard_map(local, mesh=mesh, in_specs=in_specs, out_specs=out_specs, check_vma=False)
```

time: 63.4 us -> 54.8 us (0.86)
  Pallas kernels: 57.6 us -> 49 us
    pallas_call x3 -> x1, Pallas kernels: 57.6 us -> 49 us  [local(): pl.pallas_call(kernel, out_shape=jax.ShapeDtypeStruct((CH, NH * LANES), F...]
where the time goes in v1:
time: 54.8 us; the launch traced here: 54.6 us
  Pallas kernels  49 us (89%)
  local copies, waits for them, and re-layouts  5.55 us (10%)
    pallas_call x1, Pallas kernels, local(): pl.pallas_call(kernel, out_shape=jax.ShapeDtypeStruct((CH, NH * LANES), F...  49 us
    unnamed x13, local copies, waits for them, and re-layouts  5.55 us

profile of v1, /device:TPU:0, one launch (start us, length us, event | category | flops | bytes accessed | tf_op | source)
XLA Modules:
  0.0 54.6 jit_solution(9499565634466748849)
XLA Ops:
  0.0 0.0 copy-start
  0.0 0.9 %copy-done = f32[32,2048]{1,0:T(8,128)S(1)} copy-done((f32[32,2048]{1,0:T(8,128)S(1)}, f32[32,2048]{1,0:T(8,128)}, u32[]{:S(2)}) %copy-start) | copy-done | bytes 262168
  1.0 0.0 copy-start.1
  1.0 0.9 %copy-done.1 = bf16[32,2048]{1,0:T(8,128)(2,1)S(1)} copy-done((bf16[32,2048]{1,0:T(8,128)(2,1)S(1)}, bf16[32,2048]{1,0:T(8,128)(2,1)}, u32[]{:S(2)}) %copy-start.1) | copy-done | bytes 131096
  1.9 0.0 copy-start.2
  1.9 0.9 %copy-done.2 = bf16[32,2048]{1,0:T(8,128)(2,1)S(1)} copy-done((bf16[32,2048]{1,0:T(8,128)(2,1)S(1)}, bf16[32,2048]{1,0:T(8,128)(2,1)}, u32[]{:S(2)}) %copy-start.2) | copy-done | bytes 131096
  2.8 0.0 copy-start.3
  2.8 0.8 %copy-done.3 = bf16[32,512]{1,0:T(8,128)(2,1)S(1)} copy-done((bf16[32,512]{1,0:T(8,128)(2,1)S(1)}, bf16[32,512]{1,0:T(8,128)(2,1)}, u32[]{:S(2)}) %copy-start.3) | copy-done | bytes 32792
  3.5 0.0 copy-start.4
  3.5 0.7 %copy-done.4 = s32[2,4]{1,0:T(2,128)S(1)} copy-done((s32[2,4]{1,0:T(2,128)S(1)}, s32[2,4]{1,0:T(2,128)}, u32[]{:S(2)}) %copy-start.4) | copy-done | bytes 56
  4.2 0.0 copy-start.5
  4.2 0.7 %copy-done.5 = f32[32]{0:T(128)S(1)} copy-done((f32[32]{0:T(128)S(1)}, f32[32]{0:T(128)}, u32[]{:S(2)}) %copy-start.5) | copy-done | bytes 152
  4.9 49.0 %shard_map.64 = f32[32,2048]{1,0:T(8,128)S(1)} custom-call(bf16[32,2048]{1,0:T(8,128)(2,1)S(1)} %copy-done.1, bf16[32,2048]{1,0:T(8,128)(2,1)S(1)} %copy-done.2, f32[32,2048]{1,0:T(8,128)S(1)} %copy-done, bf16[32,512]{1,0:T(8,128)(2,1)S(1)} %copy-done.3, s32[2,4]{1,0:T(2,128)S(1)} %copy-done.4, f32[32]{0:T(128)S(1)} %copy-done.5), custom_call_target="tpu_custom_call" | custom-call | tf_op jit(solution)/shard_map/pallas_call | solution.py:268
  53.9 0.7 %copy.8 = f32[32,2048]{1,0:T(8,128)} copy(f32[32,2048]{1,0:T(8,128)S(1)} %shard_map.64) | data formatting | bytes 524288
Async XLA Ops:
  0.0 0.9 %copy-start = (f32[32,2048]{1,0:T(8,128)S(1)}, f32[32,2048]{1,0:T(8,128)}, u32[]{:S(2)}) copy-start(f32[32,2048]{1,0:T(8,128)} %h_hbm.1) | copy-start | bytes 786436
  1.0 0.9 %copy-start.1 = (bf16[32,2048]{1,0:T(8,128)(2,1)S(1)}, bf16[32,2048]{1,0:T(8,128)(2,1)}, u32[]{:S(2)}) copy-start(bf16[32,2048]{1,0:T(8,128)(2,1)} %x_hbm.1) | copy-start | bytes 393220
  1.9 0.9 %copy-start.2 = (bf16[32,2048]{1,0:T(8,128)(2,1)S(1)}, bf16[32,2048]{1,0:T(8,128)(2,1)}, u32[]{:S(2)}) copy-start(bf16[32,2048]{1,0:T(8,128)(2,1)} %g_hbm.1) | copy-start | bytes 393220
  2.8 0.8 %copy-start.3 = (bf16[32,512]{1,0:T(8,128)(2,1)S(1)}, bf16[32,512]{1,0:T(8,128)(2,1)}, u32[]{:S(2)}) copy-start(bf16[32,512]{1,0:T(8,128)(2,1)} %w_hbm.1) | copy-start | bytes 98308
  3.5 0.7 %copy-start.4 = (s32[2,4]{1,0:T(2,128)S(1)}, s32[2,4]{1,0:T(2,128)}, u32[]{:S(2)}) copy-start(s32[2,4]{1,0:T(2,128)} %far_hbm.1) | copy-start | bytes 100
  4.2 0.7 %copy-start.5 = (f32[32]{0:T(128)S(1)}, f32[32]{0:T(128)}, u32[]{:S(2)}) copy-start(f32[32]{0:T(128)} %skip_hbm.1) | copy-start | bytes 388

commit v2 on v1

--- a/solution.py
+++ b/solution.py
@@ -18,6 +18,8 @@
 ROWS = 16
 PER = 3 * ROWS
 WIN = 2
+PART = 16
+TILES = 5
 MESH = pl.DeviceIdType.MESH
 
 
@@ -33,39 +35,107 @@
         )
 
 
-def shifted_taps(taps, big):
-    lane = lax.broadcasted_iota(jnp.int32, (16, LANES), 1)
-    keep = lane >= lax.broadcasted_iota(jnp.int32, (16, LANES), 0)
-    big[0] = jnp.zeros((LANES, LANES), BF16)
-
-    def step(p, carry):
-        before, edges = carry
-        row = jnp.broadcast_to(taps[pl.ds(p, 1), :], (16, LANES))
-        turned = pltpu.roll(row, 0, 1, stride=1, stride_axis=0)
-        edge = jnp.where(keep, turned, before).astype(BF16)
-        big[p + 1, 0:16, :] = edge
-        rolled = []
-        for k in range(1, 8):
-            r = pltpu.roll(edge, 16 * k, 1)
-            big[p + 1, 16 * k : 16 * k + 16, :] = jnp.where(lane >= 16 * k, r, edges[k - 1])
-            rolled.append(r)
-        return turned, tuple(rolled)
-
-    zero = jnp.zeros((16, LANES), F32)
-    lax.fori_loop(0, PIECES, step, (zero, (zero.astype(BF16),) * 7), unroll=16)
-
-
-def fill(me_c, m, got, lo, wide):
-    for c in range(NC):
-        base = pl.multiple_of(m * PER + lo, 16)
-        wide[ROWS * c : ROWS * (c + 1), :] = got[c, pl.ds(base, ROWS), :].astype(F32)
+def read_masks(far, masks):
+    block = lax.broadcasted_iota(jnp.int32, (BLOCKS, LANES), 0)
+    chunk = lax.broadcasted_iota(jnp.int32, (BLOCKS, LANES), 1) // PART
+
+    def reads(lag):
+        if lag < WIN:
+            return jnp.ones((BLOCKS, LANES), F32)
+        mask = jnp.zeros((BLOCKS, LANES), F32)
+        if lag < BLOCKS:
+            for k in range(4):
+                mask = jnp.where(far[pl.ds(k, BLOCKS, stride=4), :] == block - lag, 1.0, mask)
+        return mask
+
+    now = reads(0)
+    for d in range(BLOCKS):
+        after = reads(d + 1)
+        masks[0, d] = after
+        for a in range(1, TILES - 1):
+            masks[a, d] = jnp.where(chunk <= 2 * a - 1, now, after)
+        masks[TILES - 1, d] = now
+        now = after
+
+
+def prepare(m, read, taps, wide, turned, base, edges):
+    read(m, 1, wide)
+    read(m, 0, taps)
+    lane = lax.broadcasted_iota(jnp.int32, (PART, LANES), 1)
+    chunk = lane // PART
+    for b in range(SUBS):
+        piece = wide[pl.ds(b, BLOCKS, stride=SUBS), :]
+        for s in range(SUBS):
+            turned[b, s, BLOCKS : 2 * BLOCKS, :] = pltpu.roll(piece, PART * s, 1) if s else piece
+    for f in range(SUBS):
+        for a in range(TILES):
+            tile = None
+            for v in range(SUBS):
+                b = 2 * a - 1 - v
+                lo = BLOCKS if b >= 0 else BLOCKS - 1
+                piece = turned[b % SUBS, (v - f) % SUBS, lo : lo + BLOCKS, :]
+                tile = piece if tile is None else jnp.where(chunk == v, piece, tile)
+            base[f, a, BLOCKS : 2 * BLOCKS, :] = tile
+    keep = lane >= lax.broadcasted_iota(jnp.int32, (PART, LANES), 0)
+    before = jnp.zeros((PART, LANES), F32)
+    for p in range(PIECES):
+        row = jnp.broadcast_to(taps[p : p + 1, :], (PART, LANES))
+        turn = pltpu.roll(row, 0, 1, stride=1, stride_axis=0)
+        edges[PART * (p + 1) : PART * (p + 2), :] = jnp.where(keep, turn, before).astype(BF16)
+        before = turn
+
+
+def multiply(masks, base, edges, total):
+    for g in range(0, BLOCKS, 2):
+        left = []
+        for f in range(SUBS):
+            for a in range(TILES):
+                left.append(
+                    jnp.concatenate(
+                        [
+                            (base[f, a, BLOCKS - d : 2 * BLOCKS - d, :] * masks[a, d]).astype(BF16)
+                            for d in (g, g + 1)
+                        ],
+                        axis=1,
+                    )
+                )
+        lo = LANES * g
+        right = jnp.concatenate(
+            [edges[lo : lo + 256, :], edges[lo + PART : lo + PART + 256, :]], axis=1
+        )
+        part = jnp.dot(jnp.concatenate(left, axis=0), right, preferred_element_type=F32)
+        if g == 0:
+            total[...] = part
+        else:
+            total[...] += part
+
+
+def finish(m, read, skip, total, wide, gate, mixed):
+    read(m, 2, gate)
+    read(m, 1, wide)
+    lane = lax.broadcasted_iota(jnp.int32, (BLOCKS, LANES), 1)
+    for a in range(TILES - 1):
+        for f in range(SUBS):
+            row = BLOCKS * (TILES * f + a + 1)
+            first = total[row : row + BLOCKS, 0:LANES]
+            second = total[row : row + BLOCKS, LANES : 2 * LANES]
+            if f == 0:
+                low, high = first, second
+                continue
+            before = pltpu.roll(total[row - BLOCKS : row, LANES : 2 * LANES], PART * f, 1)
+            first, second = pltpu.roll(first, PART * f, 1), pltpu.roll(second, PART * f, 1)
+            low = low + jnp.where(lane >= PART * f, first, before)
+            high = high + jnp.where(lane >= PART * f, second, first)
+        for b, y in ((2 * a, low), (2 * a + 1, high)):
+            rows = pl.ds(b, BLOCKS, stride=SUBS)
+            mixed[rows, :] = gate[rows, :] * (y + skip * wide[rows, :])
 
 
 def kernel(
     x_hbm, g_hbm, h_hbm, w_hbm, far_hbm, skip_hbm, out,
     x_in, g_in, h_in, w_in, far_in, skip_in,
     stage, packed, got, far_mine, far_got, w_got,
-    taps, padded, wide, mixed, masks, source, big,
+    taps, wide, x_own, g_own, mixed, masks, turned, base0, edges0, total0, base1, edges1, total1,
     ready, back, regroup, sliced, part, result,
     load_sem, own_sem, in_send, in_recv, far_send, far_recv, w_send, w_recv,
     m_send, m_recv, t_send, t_recv, o_send, o_recv,
@@ -159,74 +229,62 @@
         copy.start()
     for copy in own:
         copy.wait()
-    for b in range(SUBS):
-        padded[b, 0:BLOCKS, :] = jnp.zeros((BLOCKS, LANES), F32)
-    for b in range(4):
-        source[BLOCKS, b] = jnp.zeros((BLOCKS, 256), BF16)
+    empty = jnp.zeros((BLOCKS, LANES), F32)
+    for f in range(SUBS):
+        for a in range(TILES):
+            base0[f, a, 0:BLOCKS, :] = empty
+            base1[f, a, 0:BLOCKS, :] = empty
+        for b in range(SUBS):
+            turned[b, f, 0:BLOCKS, :] = empty
+    edges0[0:PART, :] = empty.astype(BF16)
+    edges1[0:PART, :] = empty.astype(BF16)
     for k in range(1, NC):
         far_copy(k).wait()
     for c in range(NC):
         regroup[8 * c : 8 * c + 8, :] = far_got[c]
-    for d in range(BLOCKS):
-        block = lax.broadcasted_iota(jnp.int32, (BLOCKS, LANES), 0)
-        mask = jnp.full((BLOCKS, LANES), 1.0 if d < WIN else 0.0, F32)
-        if d >= WIN:
-            for k in range(4):
-                mask = jnp.where(regroup[pl.ds(k, BLOCKS, stride=4), :] == block - d, 1.0, mask)
-        masks[d] = mask
-
-    def channel(m, _):
+    read_masks(regroup, masks)
+
+    def read(m, a, to):
+        rows = pl.ds(pl.multiple_of(m * PER + a * ROWS, 16), ROWS)
+        for c in range(NC):
+            to[ROWS * c : ROWS * (c + 1), :] = got[c, rows, :].astype(F32)
+
+    def arrive(m):
         for k in range(1, NC):
             in_copy(m, k).wait()
-        fill(me_c, m, got, 0, taps)
-        fill(me_c, m, got, ROWS, wide)
-        for b in range(SUBS):
-            padded[b, BLOCKS : 2 * BLOCKS, :] = wide[pl.ds(b, BLOCKS, stride=SUBS), :]
-        for d in range(BLOCKS):
-            mask = masks[d]
-            for b in range(SUBS):
-                lo = LANES * (b % 2)
-                source[d, b // 2, :, lo : lo + LANES] = (
-                    padded[b, BLOCKS - d : 2 * BLOCKS - d, :] * mask
-                ).astype(BF16)
-        shifted_taps(taps, big)
-
-        def group(q4, acc):
-            for u in range(4):
-                rows = []
-                for a in range(4):
-                    b = (a - u) % 4
-                    rows.append(source[q4 + (u - a + b) // 4, b])
-                q = 4 * q4 + u
-                here, after, before = big[2 * q + 1], big[2 * q + 2], big[2 * q]
-                right = jnp.concatenate(
-                    [
-                        jnp.concatenate([here, after], axis=1),
-                        jnp.concatenate([before, here], axis=1),
-                    ],
-                    axis=0,
-                )
-                acc = acc + jnp.dot(
-                    jnp.concatenate(rows, axis=0), right, preferred_element_type=F32
-                )
-            return acc
-
-        acc = lax.fori_loop(0, BLOCKS, group, jnp.zeros((64, 256), F32), unroll=2)
-        fill(me_c, m, got, 2 * ROWS, wide)
-        skip = skip_in[MINE * me_c + m]
-        for b in range(SUBS):
-            a, lo = b // 2, LANES * (b % 2)
-            y = acc[16 * a : 16 * a + 16, lo : lo + LANES] + skip * padded[b, BLOCKS : 2 * BLOCKS, :]
-            mixed[pl.ds(b, BLOCKS, stride=SUBS), :] = wide[pl.ds(b, BLOCKS, stride=SUBS), :] * y
+
+    def hand_back(m, total):
+        finish(m, read, skip_in[MINE * me_c + m], total, x_own, g_own, mixed)
         for c in range(NC):
             ready[c, pl.ds(pl.multiple_of(m * ROWS, 16), ROWS), :] = mixed[
                 ROWS * c : ROWS * (c + 1), :
             ].astype(BF16)
+
+    def send_back(m):
         for k in range(1, NC):
             m_copy(m, k).start()
+
+    arrive(0)
+    prepare(0, read, taps, wide, turned, base0, edges0)
+
+    def pair(t, _):
+        arrive(2 * t + 1)
+        multiply(masks, base0, edges0, total0)
+        prepare(2 * t + 1, read, taps, wide, turned, base1, edges1)
+
+        @pl.when(t == 0)
+        def _():
+            arrive(2)
+
+        multiply(masks, base1, edges1, total1)
+        prepare(jnp.minimum(2 * t + 2, MINE - 1), read, taps, wide, turned, base0, edges0)
+        hand_back(2 * t, total0)
+        send_back(2 * t)
+        hand_back(2 * t + 1, total1)
+        send_back(2 * t + 1)
         return 0
 
-    lax.fori_loop(0, MINE, channel, 0)
+    lax.fori_loop(0, MINE // 2, pair, 0)
     copy = pltpu.make_async_copy(ready.at[me_c], back.at[me_c], own_sem.at[3])
     copy.start()
     copy.wait()
@@ -279,13 +337,15 @@
             vmem((8, LANES), jnp.int32),
             vmem((NC, 8, LANES), jnp.int32),
             vmem((NH, CH, NH * CH), BF16),
-            vmem((PIECES, LANES), F32),
-            vmem((SUBS, 2 * BLOCKS, LANES), F32),
-            vmem((PIECES, LANES), F32),
-            vmem((PIECES, LANES), F32),
-            vmem((BLOCKS, BLOCKS, LANES), F32),
-            vmem((BLOCKS + 1, 4, BLOCKS, 256), BF16),
-            vmem((PIECES + 1, LANES, LANES), BF16),
+            *[vmem((PIECES, LANES), F32)] * 5,
+            vmem((TILES, BLOCKS, BLOCKS, LANES), F32),
+            vmem((SUBS, SUBS, 2 * BLOCKS, LANES), F32),
+            *[
+                vmem((SUBS, TILES, 2 * BLOCKS, LANES), F32),
+                vmem((PART * (PIECES + 1), LANES), BF16),
+                vmem((SUBS * TILES * BLOCKS, 2 * LANES), F32),
+            ]
+            * 2,
             vmem((NC, MINE * ROWS, LANES), BF16),
             vmem((NC, MINE * ROWS, LANES), BF16),
             vmem((NC * 8, LANES), jnp.int32),
@@ -297,7 +357,7 @@
             dma((NH,)), dma((NH,)), dma((NH,)), dma((NH,)),
         ],
         compiler_params=pltpu.CompilerParams(
-            collective_id=0, has_side_effects=True, vmem_limit_bytes=40 << 20
+            collective_id=0, has_side_effects=True, vmem_limit_bytes=62 << 20
         ),
     )(inputs, gate, filter_taps, w_out, far_pairs, skip)
 

time: 54.8 us -> 38.1 us (0.70)
  Pallas kernels: 49 us -> 36.3 us
  local copies, waits for them, and re-layouts: 5.55 us -> 1.67 us
    pallas_call x1, Pallas kernels: 49 us -> 36.3 us  [local(): pl.pallas_call(kernel, out_shape=jax.ShapeDtypeStruct((CH, NH * LANES), F...]
    unnamed x13 -> x1, local copies, waits for them, and re-layouts: 5.55 us -> 1.67 us
where the time goes in v2:
time: 38.1 us; the launch traced here: 37.9 us
  Pallas kernels  36.3 us (95%)
  local copies, waits for them, and re-layouts  1.67 us (4%)
    pallas_call x1, Pallas kernels, local(): pl.pallas_call(kernel, out_shape=jax.ShapeDtypeStruct((CH, NH * LANES), F...  36.3 us
    unnamed x1, local copies, waits for them, and re-layouts  1.67 us

profile of v2, /device:TPU:0, one launch (start us, length us, event | category | flops | bytes accessed | tf_op | source)
XLA Modules:
  0.0 37.9 jit_solution(17818821078281550207)
XLA Ops:
  0.0 36.3 %shard_map.64 = f32[32,2048]{1,0:T(8,128)} custom-call(bf16[32,2048]{1,0:T(8,128)(2,1)} %x_hbm.1, bf16[32,2048]{1,0:T(8,128)(2,1)} %g_hbm.1, f32[32,2048]{1,0:T(8,128)} %h_hbm.1, bf16[32,512]{1,0:T(8,128)(2,1)} %w_hbm.1, s32[2,4]{1,0:T(2,128)} %far_hbm.1, f32[32]{0:T(128)} %skip_hbm.1), custom_call_target="tpu_custom_call" | custom-call | tf_op jit(solution)/shard_map/pallas_call | solution.py:326
  36.3 1.7 %copy.8 = f32[32,2048]{1,0:T(8,128)} copy(f32[32,2048]{1,0:T(8,128)} %shard_map.64) | data formatting | bytes 524288

commit v3 on v2

--- a/solution.py
+++ b/solution.py
@@ -16,7 +16,8 @@
 CH = 32
 MINE = CH // NC
 ROWS = 16
-PER = 3 * ROWS
+PER = 2 * ROWS
+GATES = MINE * PER
 WIN = 2
 PART = 16
 TILES = 5
@@ -137,7 +138,7 @@
     stage, packed, got, far_mine, far_got, w_got,
     taps, wide, x_own, g_own, mixed, masks, turned, base0, edges0, total0, base1, edges1, total1,
     ready, back, regroup, sliced, part, result,
-    load_sem, own_sem, in_send, in_recv, far_send, far_recv, w_send, w_recv,
+    w_wide, w_sorted, load_sem, own_sem, in_send, in_recv, g_send, g_recv, far_send, far_recv, w_send, w_recv,
     m_send, m_recv, t_send, t_recv, o_send, o_recv,
 ):
     me_c, me_h = lax.axis_index("ctx"), lax.axis_index("head")
@@ -153,7 +154,7 @@
         return remote(far_mine, far_got.at[me_c], far_send.at[k], far_recv.at[k], "ctx", k)
 
     def w_copy(k):
-        return remote(w_in, w_got.at[me_h], w_send.at[k], w_recv.at[k], "head", k)
+        return remote(w_sorted, w_got.at[me_h], w_send.at[k], w_recv.at[k], "head", k)
 
     def in_copy(m, k):
         rows = pl.ds(pl.multiple_of(m * PER, 16), PER)
@@ -162,6 +163,13 @@
             packed.at[peer, rows], got.at[me_c, rows], in_send.at[m, k], in_recv.at[m, k], "ctx", k
         )
 
+    def gate_copy(k):
+        rows = pl.ds(GATES, MINE * ROWS)
+        peer = lax.rem(me_c + k, NC)
+        return remote(
+            packed.at[peer, rows], got.at[me_c, rows], g_send.at[k], g_recv.at[k], "ctx", k
+        )
+
     def m_copy(m, k):
         rows = pl.ds(pl.multiple_of(m * ROWS, 16), ROWS)
         peer = lax.rem(me_c + k, NC)
@@ -169,9 +177,11 @@
             ready.at[peer, rows], back.at[me_c, rows], m_send.at[m, k], m_recv.at[m, k], "ctx", k
         )
 
-    def t_copy(k):
+    def t_copy(t, k):
         peer = lax.rem(me_h + k, NH)
-        return remote(sliced.at[peer], part.at[me_h], t_send.at[k], t_recv.at[k], "head", k)
+        return remote(
+            sliced.at[t, peer], part.at[t, me_h], t_send.at[t, k], t_recv.at[t, k], "head", k
+        )
 
     columns = pl.ds(pl.multiple_of(me_h * LANES, LANES), LANES)
 
@@ -191,7 +201,25 @@
     for copy in loads:
         copy.start()
     greet(me_c, me_h)
-    for copy in loads:
+
+    def pack(a, ref):
+        for s in range(ROWS):
+            stage[a, pl.ds(s, CH, stride=ROWS), :] = ref[:, LANES * s : LANES * (s + 1)].astype(F32)
+        for c in range(NC):
+            for m in range(MINE):
+                ch = MINE * c + m
+                lo = PER * m + ROWS * a if a < 2 else GATES + ROWS * m
+                packed[c, lo : lo + ROWS, :] = stage[a, ROWS * ch : ROWS * (ch + 1), :].astype(BF16)
+
+    loads[0].wait()
+    pack(0, h_in)
+    loads[1].wait()
+    pack(1, x_in)
+    pl.semaphore_wait(pltpu.get_barrier_semaphore(), NC - 1 + NH - 1)
+    for m in range(MINE):
+        for k in range(1, NC):
+            in_copy(m, k).start()
+    for copy in loads[2:]:
         copy.wait()
     row = lax.broadcasted_iota(jnp.int32, (8, LANES), 0)
     table = jnp.full((8, LANES), -1, jnp.int32)
@@ -199,29 +227,25 @@
         for k in range(4):
             table = jnp.where(row == 4 * r + k, far_in[r, k], table)
     far_mine[...] = table
-    for a, ref in enumerate((h_in, x_in, g_in)):
-        for s in range(ROWS):
-            stage[a, pl.ds(s, CH, stride=ROWS), :] = ref[:, LANES * s : LANES * (s + 1)].astype(F32)
-        for c in range(NC):
-            for m in range(MINE):
-                ch = MINE * c + m
-                packed[c, PER * m + ROWS * a : PER * m + ROWS * (a + 1), :] = stage[
-                    a, ROWS * ch : ROWS * (ch + 1), :
-                ].astype(BF16)
-    pl.semaphore_wait(pltpu.get_barrier_semaphore(), NC - 1 + NH - 1)
-
     for k in range(1, NC):
         far_copy(k).start()
-    for m in range(MINE):
-        for k in range(1, NC):
-            in_copy(m, k).start()
+    pack(2, g_in)
+    for k in range(1, NC):
+        gate_copy(k).start()
+    for j in range(4):
+        w_wide[j] = w_in[:, LANES * j : LANES * (j + 1)].astype(F32)
+        for m in range(0, MINE, 2):
+            rows = [w_wide[j, pl.ds(m + i, NC, stride=MINE), :] for i in range(2)]
+            w_sorted[NC * m : NC * (m + 2), LANES * j : LANES * (j + 1)] = jnp.concatenate(
+                rows, axis=0
+            ).astype(BF16)
     for k in range(1, NH):
         w_copy(k).start()
     own = [
         pltpu.make_async_copy(a, b, own_sem.at[i])
         for i, (a, b) in enumerate(
             (
-                (far_mine, far_got.at[me_c]), (packed.at[me_c], got.at[me_c]), (w_in, w_got.at[me_h]),
+                (far_mine, far_got.at[me_c]), (packed.at[me_c], got.at[me_c]), (w_sorted, w_got.at[me_h]),
             )
         )
     ]
@@ -245,7 +269,8 @@
     read_masks(regroup, masks)
 
     def read(m, a, to):
-        rows = pl.ds(pl.multiple_of(m * PER + a * ROWS, 16), ROWS)
+        lo = m * PER + a * ROWS if a < 2 else GATES + m * ROWS
+        rows = pl.ds(pl.multiple_of(lo, 16), ROWS)
         for c in range(NC):
             to[ROWS * c : ROWS * (c + 1), :] = got[c, rows, :].astype(F32)
 
@@ -264,6 +289,23 @@
         for k in range(1, NC):
             m_copy(m, k).start()
 
+    def pass_on(t):
+        for m in (2 * t, 2 * t + 1):
+            for k in range(1, NC):
+                m_copy(m, k).wait()
+        for c in range(NC):
+            for i in range(2):
+                stage[0, ROWS * (2 * c + i) : ROWS * (2 * c + i + 1), :] = jnp.where(
+                    me_c == c,
+                    ready[c, ROWS * (2 * t + i) : ROWS * (2 * t + i + 1), :].astype(F32),
+                    back[c, ROWS * (2 * t + i) : ROWS * (2 * t + i + 1), :].astype(F32),
+                )
+        for h in range(NH):
+            rows = [stage[0, pl.ds(ROWS * i + h, NC, stride=2 * ROWS), :] for i in range(2)]
+            sliced[t, h] = jnp.concatenate(rows, axis=0).astype(BF16)
+        for k in range(1, NH):
+            t_copy(t, k).start()
+
     arrive(0)
     prepare(0, read, taps, wide, turned, base0, edges0)
 
@@ -275,6 +317,12 @@
         @pl.when(t == 0)
         def _():
             arrive(2)
+            for k in range(1, NC):
+                gate_copy(k).wait()
+
+        @pl.when(t == 1)
+        def _():
+            pass_on(0)
 
         multiply(masks, base1, edges1, total1)
         prepare(jnp.minimum(2 * t + 2, MINE - 1), read, taps, wide, turned, base0, edges0)
@@ -285,29 +333,24 @@
         return 0
 
     lax.fori_loop(0, MINE // 2, pair, 0)
-    copy = pltpu.make_async_copy(ready.at[me_c], back.at[me_c], own_sem.at[3])
-    copy.start()
-    copy.wait()
-    for m in range(MINE):
-        for k in range(1, NC):
-            m_copy(m, k).wait()
-    for c in range(NC):
-        stage[0, 64 * c : 64 * c + 64, :] = back[c].astype(F32)
-    for t in range(NH):
-        sliced[t] = stage[0, pl.ds(t, CH, stride=NH), :].astype(BF16)
-    for k in range(1, NH):
-        t_copy(k).start()
-    copy = pltpu.make_async_copy(sliced.at[me_h], part.at[me_h], own_sem.at[4])
-    copy.start()
-    copy.wait()
+    pass_on(1)
+    for t in range(2):
+        copy = pltpu.make_async_copy(sliced.at[t, me_h], part.at[t, me_h], own_sem.at[3 + t])
+        copy.start()
+        copy.wait()
     for k in range(1, NH):
         w_copy(k).wait()
-    for k in range(1, NH):
-        t_copy(k).wait()
-    total = lax.dot_general(
-        w_got[...].reshape(NH * CH, NH * CH), part[...].reshape(NH * CH, LANES),
-        (((0,), (0,)), ((), ())), preferred_element_type=F32,
-    )
+    total = None
+    for t in range(2):
+        for k in range(1, NH):
+            t_copy(t, k).wait()
+        half = lax.dot_general(
+            w_got[:, 16 * t : 16 * t + 16, :].reshape(NH * 16, NH * CH),
+            part[t].reshape(NH * 16, LANES),
+            (((0,), (0,)), ((), ())),
+            preferred_element_type=F32,
+        )
+        total = half if t == 0 else total + half
     for t in range(NH):
         result[t] = total[CH * t : CH * (t + 1), :]
     for k in range(1, NH):
@@ -323,6 +366,7 @@
     hbm = pl.BlockSpec(memory_space=pltpu.HBM)
     dma = pltpu.SemaphoreType.DMA
     vmem = pltpu.VMEM
+    arrays = (inputs, gate, filter_taps, w_out, far_pairs, skip)
     return pl.pallas_call(
         kernel,
         out_shape=jax.ShapeDtypeStruct((CH, NH * LANES), F32),
@@ -332,8 +376,8 @@
             vmem(inputs.shape, BF16), vmem(gate.shape, BF16), vmem(filter_taps.shape, F32),
             vmem(w_out.shape, BF16), pltpu.SMEM(far_pairs.shape, jnp.int32), pltpu.SMEM(skip.shape, F32),
             vmem((3, CH * ROWS, LANES), F32),
-            vmem((NC, MINE * PER, LANES), BF16),
-            vmem((NC, MINE * PER, LANES), BF16),
+            vmem((NC, GATES + MINE * ROWS, LANES), BF16),
+            vmem((NC, GATES + MINE * ROWS, LANES), BF16),
             vmem((8, LANES), jnp.int32),
             vmem((NC, 8, LANES), jnp.int32),
             vmem((NH, CH, NH * CH), BF16),
@@ -349,17 +393,19 @@
             vmem((NC, MINE * ROWS, LANES), BF16),
             vmem((NC, MINE * ROWS, LANES), BF16),
             vmem((NC * 8, LANES), jnp.int32),
-            vmem((NH, CH, LANES), BF16),
-            vmem((NH, CH, LANES), BF16),
+            vmem((2, NH, 16, LANES), BF16),
+            vmem((2, NH, 16, LANES), BF16),
             vmem((NH, CH, LANES), F32),
+            vmem((4, CH, LANES), F32),
+            vmem((CH, NH * CH), BF16),
             dma((6,)), dma((6,)), dma((MINE, NC)), dma((MINE, NC)), dma((NC,)), dma((NC,)),
-            dma((NH,)), dma((NH,)), dma((MINE, NC)), dma((MINE, NC)),
-            dma((NH,)), dma((NH,)), dma((NH,)), dma((NH,)),
+            dma((NC,)), dma((NC,)), dma((NH,)), dma((NH,)), dma((MINE, NC)), dma((MINE, NC)),
+            dma((2, NH)), dma((2, NH)), dma((NH,)), dma((NH,)),
         ],
         compiler_params=pltpu.CompilerParams(
-            collective_id=0, has_side_effects=True, vmem_limit_bytes=62 << 20
+            collective_id=0, has_side_effects=True, vmem_limit_bytes=40 << 20
         ),
-    )(inputs, gate, filter_taps, w_out, far_pairs, skip)
+    )(*(pltpu.with_memory_space_constraint(a, pltpu.HBM) for a in arrays))
 
 
 def solution(mesh):

time: 38.1 us -> 40.6 us (1.066)
  Pallas kernels: 36.3 us -> 39.8 us
  local copies, waits for them, and re-layouts: 1.67 us -> 0.71 us
    pallas_call x1, Pallas kernels: 36.3 us -> 39.8 us  [local(): pl.pallas_call(kernel, out_shape=jax.ShapeDtypeStruct((CH, NH * LANES), F...]
    unnamed x1, local copies, waits for them, and re-layouts: 1.67 us -> 0.71 us
where the time goes in v3:
time: 40.6 us; the launch traced here: 40.5 us
  Pallas kernels  39.8 us (98%)
  local copies, waits for them, and re-layouts  0.71 us (2%)
    pallas_call x1, Pallas kernels, local(): pl.pallas_call(kernel, out_shape=jax.ShapeDtypeStruct((CH, NH * LANES), F...  39.8 us

profile of v3, /device:TPU:0, one launch (start us, length us, event | category | flops | bytes accessed | tf_op | source)
XLA Modules:
  0.0 40.5 jit_solution(12385805339915986235)
XLA Ops:
  0.0 39.8 %shard_map.64 = f32[32,2048]{1,0:T(8,128)S(1)} custom-call(bf16[32,2048]{1,0:T(8,128)(2,1)} %x_hbm.1, bf16[32,2048]{1,0:T(8,128)(2,1)} %g_hbm.1, f32[32,2048]{1,0:T(8,128)} %h_hbm.1, bf16[32,512]{1,0:T(8,128)(2,1)} %w_hbm.1, s32[2,4]{1,0:T(2,128)} %far_hbm.1, f32[32]{0:T(128)} %skip_hbm.1), custom_call_target="tpu_custom_call" | custom-call | tf_op jit(solution)/shard_map/pallas_call | solution.py:370
  39.8 0.7 %copy.8 = f32[32,2048]{1,0:T(8,128)} copy(f32[32,2048]{1,0:T(8,128)S(1)} %shard_map.64) | data formatting | bytes 524288

commit v4 on v2

--- a/solution.py
+++ b/solution.py
@@ -16,7 +16,10 @@
 CH = 32
 MINE = CH // NC
 ROWS = 16
-PER = 3 * ROWS
+PER = 2 * ROWS
+TAPS = ROWS
+GATES = TAPS + MINE * PER
+LEGS = ((0, TAPS + PER), (TAPS + PER, (MINE - 1) * PER), (GATES, MINE * ROWS))
 WIN = 2
 PART = 16
 TILES = 5
@@ -36,7 +39,7 @@
 
 
 def read_masks(far, masks):
-    block = lax.broadcasted_iota(jnp.int32, (BLOCKS, LANES), 0)
+    block = lax.broadcasted_iota(jnp.int32, (BLOCKS, LANES), 0).astype(F32)
     chunk = lax.broadcasted_iota(jnp.int32, (BLOCKS, LANES), 1) // PART
 
     def reads(lag):
@@ -134,10 +137,10 @@
 def kernel(
     x_hbm, g_hbm, h_hbm, w_hbm, far_hbm, skip_hbm, out,
     x_in, g_in, h_in, w_in, far_in, skip_in,
-    stage, packed, got, far_mine, far_got, w_got,
+    stage, packed, got, w_got,
     taps, wide, x_own, g_own, mixed, masks, turned, base0, edges0, total0, base1, edges1, total1,
     ready, back, regroup, sliced, part, result,
-    load_sem, own_sem, in_send, in_recv, far_send, far_recv, w_send, w_recv,
+    load_sem, own_sem, in_send, in_recv, w_send, w_recv,
     m_send, m_recv, t_send, t_recv, o_send, o_recv,
 ):
     me_c, me_h = lax.axis_index("ctx"), lax.axis_index("head")
@@ -149,24 +152,21 @@
             device_id={axis: lax.rem(me + k, n)}, device_id_type=MESH,
         )
 
-    def far_copy(k):
-        return remote(far_mine, far_got.at[me_c], far_send.at[k], far_recv.at[k], "ctx", k)
-
     def w_copy(k):
         return remote(w_in, w_got.at[me_h], w_send.at[k], w_recv.at[k], "head", k)
 
-    def in_copy(m, k):
-        rows = pl.ds(pl.multiple_of(m * PER, 16), PER)
+    def in_copy(leg, k):
+        rows = pl.ds(*LEGS[leg])
         peer = lax.rem(me_c + k, NC)
         return remote(
-            packed.at[peer, rows], got.at[me_c, rows], in_send.at[m, k], in_recv.at[m, k], "ctx", k
-        )
-
-    def m_copy(m, k):
-        rows = pl.ds(pl.multiple_of(m * ROWS, 16), ROWS)
+            packed.at[peer, rows], got.at[me_c, rows], in_send.at[leg, k], in_recv.at[leg, k], "ctx", k
+        )
+
+    def m_copy(t, k):
+        rows = pl.ds(pl.multiple_of(t * 2 * ROWS, 16), 2 * ROWS)
         peer = lax.rem(me_c + k, NC)
         return remote(
-            ready.at[peer, rows], back.at[me_c, rows], m_send.at[m, k], m_recv.at[m, k], "ctx", k
+            ready.at[peer, rows], back.at[me_c, rows], m_send.at[t, k], m_recv.at[t, k], "ctx", k
         )
 
     def t_copy(k):
@@ -179,49 +179,65 @@
         peer = lax.rem(me_h + k, NH)
         return remote(result.at[peer], out.at[:, columns], o_send.at[k], o_recv.at[k], "head", k)
 
+    greet(me_c, me_h)
     loads = [
         pltpu.make_async_copy(a, b, load_sem.at[i])
         for i, (a, b) in enumerate(
             (
-                (h_hbm, h_in), (x_hbm, x_in), (g_hbm, g_in), (far_hbm, far_in),
+                (h_hbm, h_in), (x_hbm, x_in), (far_hbm, far_in), (g_hbm, g_in),
                 (skip_hbm, skip_in), (w_hbm, w_in),
             )
         )
     ]
     for copy in loads:
         copy.start()
-    greet(me_c, me_h)
-    for copy in loads:
-        copy.wait()
-    row = lax.broadcasted_iota(jnp.int32, (8, LANES), 0)
-    table = jnp.full((8, LANES), -1, jnp.int32)
+
+    def spread(a, ref):
+        for s in range(ROWS):
+            stage[a, pl.ds(s, CH, stride=ROWS), :] = ref[:, LANES * s : LANES * (s + 1)].astype(F32)
+
+    def pack(a, m):
+        lo = TAPS + PER * m + ROWS * a if a < 2 else GATES + ROWS * m
+        for c in range(NC):
+            ch = MINE * c + m
+            packed[c, lo : lo + ROWS, :] = stage[a, ROWS * ch : ROWS * (ch + 1), :].astype(BF16)
+
+    def depart(leg):
+        for k in range(1, NC):
+            in_copy(leg, k).start()
+
+    loads[2].wait()
+    row = lax.broadcasted_iota(jnp.int32, (ROWS, LANES), 0)
+    table = jnp.full((ROWS, LANES), -1, jnp.int32)
     for r in range(2):
         for k in range(4):
             table = jnp.where(row == 4 * r + k, far_in[r, k], table)
-    far_mine[...] = table
-    for a, ref in enumerate((h_in, x_in, g_in)):
-        for s in range(ROWS):
-            stage[a, pl.ds(s, CH, stride=ROWS), :] = ref[:, LANES * s : LANES * (s + 1)].astype(F32)
-        for c in range(NC):
-            for m in range(MINE):
-                ch = MINE * c + m
-                packed[c, PER * m + ROWS * a : PER * m + ROWS * (a + 1), :] = stage[
-                    a, ROWS * ch : ROWS * (ch + 1), :
-                ].astype(BF16)
+    table = table.astype(F32).astype(BF16)
+    for c in range(NC):
+        packed[c, 0:ROWS, :] = table
+    for a in range(2):
+        loads[a].wait()
+        spread(a, (h_in, x_in)[a])
+        pack(a, 0)
     pl.semaphore_wait(pltpu.get_barrier_semaphore(), NC - 1 + NH - 1)
-
-    for k in range(1, NC):
-        far_copy(k).start()
+    depart(0)
+    for a in range(2):
+        for m in range(1, MINE):
+            pack(a, m)
+    depart(1)
+    for copy in loads[3:]:
+        copy.wait()
+    spread(2, g_in)
     for m in range(MINE):
-        for k in range(1, NC):
-            in_copy(m, k).start()
+        pack(2, m)
+    depart(2)
     for k in range(1, NH):
         w_copy(k).start()
     own = [
         pltpu.make_async_copy(a, b, own_sem.at[i])
         for i, (a, b) in enumerate(
             (
-                (far_mine, far_got.at[me_c]), (packed.at[me_c], got.at[me_c]), (w_in, w_got.at[me_h]),
+                (packed.at[me_c], got.at[me_c]), (w_in, w_got.at[me_h]),
             )
         )
     ]
@@ -238,20 +254,21 @@
             turned[b, f, 0:BLOCKS, :] = empty
     edges0[0:PART, :] = empty.astype(BF16)
     edges1[0:PART, :] = empty.astype(BF16)
-    for k in range(1, NC):
-        far_copy(k).wait()
+
+    def arrive(leg):
+        for k in range(1, NC):
+            in_copy(leg, k).wait()
+
+    arrive(0)
     for c in range(NC):
-        regroup[8 * c : 8 * c + 8, :] = far_got[c]
+        regroup[8 * c : 8 * c + 8, :] = got[c, 0:ROWS, :].astype(F32)[0:8]
     read_masks(regroup, masks)
 
     def read(m, a, to):
-        rows = pl.ds(pl.multiple_of(m * PER + a * ROWS, 16), ROWS)
+        lo = TAPS + m * PER + a * ROWS if a < 2 else GATES + m * ROWS
+        rows = pl.ds(pl.multiple_of(lo, 16), ROWS)
         for c in range(NC):
             to[ROWS * c : ROWS * (c + 1), :] = got[c, rows, :].astype(F32)
-
-    def arrive(m):
-        for k in range(1, NC):
-            in_copy(m, k).wait()
 
     def hand_back(m, total):
         finish(m, read, skip_in[MINE * me_c + m], total, x_own, g_own, mixed)
@@ -260,15 +277,17 @@
                 ROWS * c : ROWS * (c + 1), :
             ].astype(BF16)
 
-    def send_back(m):
+    def send_back(t):
         for k in range(1, NC):
-            m_copy(m, k).start()
-
-    arrive(0)
+            m_copy(t, k).start()
+
     prepare(0, read, taps, wide, turned, base0, edges0)
 
     def pair(t, _):
-        arrive(2 * t + 1)
+        @pl.when(t == 0)
+        def _():
+            arrive(1)
+
         multiply(masks, base0, edges0, total0)
         prepare(2 * t + 1, read, taps, wide, turned, base1, edges1)
 
@@ -279,25 +298,23 @@
         multiply(masks, base1, edges1, total1)
         prepare(jnp.minimum(2 * t + 2, MINE - 1), read, taps, wide, turned, base0, edges0)
         hand_back(2 * t, total0)
-        send_back(2 * t)
         hand_back(2 * t + 1, total1)
-        send_back(2 * t + 1)
+        send_back(t)
         return 0
 
     lax.fori_loop(0, MINE // 2, pair, 0)
-    copy = pltpu.make_async_copy(ready.at[me_c], back.at[me_c], own_sem.at[3])
-    copy.start()
-    copy.wait()
-    for m in range(MINE):
+    for t in range(2):
         for k in range(1, NC):
-            m_copy(m, k).wait()
+            m_copy(t, k).wait()
     for c in range(NC):
-        stage[0, 64 * c : 64 * c + 64, :] = back[c].astype(F32)
+        stage[0, 64 * c : 64 * c + 64, :] = jnp.where(
+            me_c == c, ready[c].astype(F32), back[c].astype(F32)
+        )
     for t in range(NH):
         sliced[t] = stage[0, pl.ds(t, CH, stride=NH), :].astype(BF16)
     for k in range(1, NH):
         t_copy(k).start()
-    copy = pltpu.make_async_copy(sliced.at[me_h], part.at[me_h], own_sem.at[4])
+    copy = pltpu.make_async_copy(sliced.at[me_h], part.at[me_h], own_sem.at[3])
     copy.start()
     copy.wait()
     for k in range(1, NH):
@@ -323,6 +340,7 @@
     hbm = pl.BlockSpec(memory_space=pltpu.HBM)
     dma = pltpu.SemaphoreType.DMA
     vmem = pltpu.VMEM
+    arrays = (inputs, gate, filter_taps, w_out, far_pairs, skip)
     return pl.pallas_call(
         kernel,
         out_shape=jax.ShapeDtypeStruct((CH, NH * LANES), F32),
@@ -332,10 +350,8 @@
             vmem(inputs.shape, BF16), vmem(gate.shape, BF16), vmem(filter_taps.shape, F32),
             vmem(w_out.shape, BF16), pltpu.SMEM(far_pairs.shape, jnp.int32), pltpu.SMEM(skip.shape, F32),
             vmem((3, CH * ROWS, LANES), F32),
-            vmem((NC, MINE * PER, LANES), BF16),
-            vmem((NC, MINE * PER, LANES), BF16),
-            vmem((8, LANES), jnp.int32),
-            vmem((NC, 8, LANES), jnp.int32),
+            vmem((NC, GATES + MINE * ROWS, LANES), BF16),
+            vmem((NC, GATES + MINE * ROWS, LANES), BF16),
             vmem((NH, CH, NH * CH), BF16),
             *[vmem((PIECES, LANES), F32)] * 5,
             vmem((TILES, BLOCKS, BLOCKS, LANES), F32),
@@ -348,18 +364,17 @@
             * 2,
             vmem((NC, MINE * ROWS, LANES), BF16),
             vmem((NC, MINE * ROWS, LANES), BF16),
-            vmem((NC * 8, LANES), jnp.int32),
+            vmem((NC * 8, LANES), F32),
             vmem((NH, CH, LANES), BF16),
             vmem((NH, CH, LANES), BF16),
             vmem((NH, CH, LANES), F32),
-            dma((6,)), dma((6,)), dma((MINE, NC)), dma((MINE, NC)), dma((NC,)), dma((NC,)),
-            dma((NH,)), dma((NH,)), dma((MINE, NC)), dma((MINE, NC)),
-            dma((NH,)), dma((NH,)), dma((NH,)), dma((NH,)),
+            dma((6,)), dma((6,)), dma((3, NC)), dma((3, NC)), dma((NH,)), dma((NH,)),
+            dma((2, NC)), dma((2, NC)), dma((NH,)), dma((NH,)), dma((NH,)), dma((NH,)),
         ],
         compiler_params=pltpu.CompilerParams(
-            collective_id=0, has_side_effects=True, vmem_limit_bytes=62 << 20
+            collective_id=0, has_side_effects=True, vmem_limit_bytes=40 << 20
         ),
-    )(inputs, gate, filter_taps, w_out, far_pairs, skip)
+    )(*(pltpu.with_memory_space_constraint(a, pltpu.HBM) for a in arrays))
 
 
 def solution(mesh):

time: 38.1 us -> 36.8 us (0.966)
  local copies, waits for them, and re-layouts: 1.67 us -> 0.71 us
  Pallas kernels: 36.3 us -> 35.9 us
    unnamed x1, local copies, waits for them, and re-layouts: 1.67 us -> 0.71 us
where the time goes in v4:
time: 36.8 us; the launch traced here: 36.6 us
  Pallas kernels  35.9 us (98%)
  local copies, waits for them, and re-layouts  0.71 us (2%)
    pallas_call x1, Pallas kernels, local(): pl.pallas_call(kernel, out_shape=jax.ShapeDtypeStruct((CH, NH * LANES), F...  35.9 us

profile of v4, /device:TPU:0, one launch (start us, length us, event | category | flops | bytes accessed | tf_op | source)
XLA Modules:
  0.0 36.6 jit_solution(11501184015421431565)
XLA Ops:
  0.0 35.9 %shard_map.64 = f32[32,2048]{1,0:T(8,128)S(1)} custom-call(bf16[32,2048]{1,0:T(8,128)(2,1)} %x_hbm.1, bf16[32,2048]{1,0:T(8,128)(2,1)} %g_hbm.1, f32[32,2048]{1,0:T(8,128)} %h_hbm.1, bf16[32,512]{1,0:T(8,128)(2,1)} %w_hbm.1, s32[2,4]{1,0:T(2,128)} %far_hbm.1, f32[32]{0:T(128)} %skip_hbm.1), custom_call_target="tpu_custom_call" | custom-call | tf_op jit(solution)/shard_map/pallas_call | solution.py:344
  35.9 0.7 %copy.8 = f32[32,2048]{1,0:T(8,128)} copy(f32[32,2048]{1,0:T(8,128)S(1)} %shard_map.64) | data formatting | bytes 524288

commit v5 on v4

--- a/solution.py
+++ b/solution.py
@@ -19,7 +19,7 @@
 PER = 2 * ROWS
 TAPS = ROWS
 GATES = TAPS + MINE * PER
-LEGS = ((0, TAPS + PER), (TAPS + PER, (MINE - 1) * PER), (GATES, MINE * ROWS))
+LEGS = ((0, TAPS + 2 * PER), (TAPS + 2 * PER, 2 * PER), (GATES, MINE * ROWS))
 WIN = 2
 PART = 16
 TILES = 5
@@ -219,10 +219,11 @@
         loads[a].wait()
         spread(a, (h_in, x_in)[a])
         pack(a, 0)
+        pack(a, 1)
     pl.semaphore_wait(pltpu.get_barrier_semaphore(), NC - 1 + NH - 1)
     depart(0)
     for a in range(2):
-        for m in range(1, MINE):
+        for m in range(2, MINE):
             pack(a, m)
     depart(1)
     for copy in loads[3:]:
@@ -283,26 +284,21 @@
 
     prepare(0, read, taps, wide, turned, base0, edges0)
 
-    def pair(t, _):
-        @pl.when(t == 0)
-        def _():
-            arrive(1)
-
-        multiply(masks, base0, edges0, total0)
-        prepare(2 * t + 1, read, taps, wide, turned, base1, edges1)
-
-        @pl.when(t == 0)
-        def _():
-            arrive(2)
-
-        multiply(masks, base1, edges1, total1)
-        prepare(jnp.minimum(2 * t + 2, MINE - 1), read, taps, wide, turned, base0, edges0)
-        hand_back(2 * t, total0)
-        hand_back(2 * t + 1, total1)
-        send_back(t)
-        return 0
-
-    lax.fori_loop(0, MINE // 2, pair, 0)
+    multiply(masks, base0, edges0, total0)
+    prepare(1, read, taps, wide, turned, base1, edges1)
+    arrive(1)
+    arrive(2)
+    multiply(masks, base1, edges1, total1)
+    prepare(2, read, taps, wide, turned, base0, edges0)
+    hand_back(0, total0)
+    multiply(masks, base0, edges0, total0)
+    prepare(3, read, taps, wide, turned, base1, edges1)
+    hand_back(1, total1)
+    send_back(0)
+    multiply(masks, base1, edges1, total1)
+    hand_back(2, total0)
+    hand_back(3, total1)
+    send_back(1)
     for t in range(2):
         for k in range(1, NC):
             m_copy(t, k).wait()

time: 36.8 us -> 35 us (0.951)
  Pallas kernels: 35.9 us -> 34.2 us
    pallas_call x1, Pallas kernels: 35.9 us -> 34.2 us  [local(): pl.pallas_call(kernel, out_shape=jax.ShapeDtypeStruct((CH, NH * LANES), F...]
where the time goes in v5:
time: 35 us; the launch traced here: 34.9 us
  Pallas kernels  34.2 us (98%)
  local copies, waits for them, and re-layouts  0.71 us (2%)
    pallas_call x1, Pallas kernels, local(): pl.pallas_call(kernel, out_shape=jax.ShapeDtypeStruct((CH, NH * LANES), F...  34.2 us
    unnamed x1, local copies, waits for them, and re-layouts  0.71 us

profile of v5, /device:TPU:0, one launch (start us, length us, event | category | flops | bytes accessed | tf_op | source)
XLA Modules:
  0.0 34.9 jit_solution(11051638427927160775)
XLA Ops:
  0.0 34.2 %shard_map.64 = f32[32,2048]{1,0:T(8,128)S(1)} custom-call(bf16[32,2048]{1,0:T(8,128)(2,1)} %x_hbm.1, bf16[32,2048]{1,0:T(8,128)(2,1)} %g_hbm.1, f32[32,2048]{1,0:T(8,128)} %h_hbm.1, bf16[32,512]{1,0:T(8,128)(2,1)} %w_hbm.1, s32[2,4]{1,0:T(2,128)} %far_hbm.1, f32[32]{0:T(128)} %skip_hbm.1), custom_call_target="tpu_custom_call" | custom-call | tf_op jit(solution)/shard_map/pallas_call | solution.py:340
  34.2 0.7 %copy.8 = f32[32,2048]{1,0:T(8,128)} copy(f32[32,2048]{1,0:T(8,128)S(1)} %shard_map.64) | data formatting | bytes 524288

commit v6 on v5

--- a/solution.py
+++ b/solution.py
@@ -72,6 +72,8 @@
             turned[b, s, BLOCKS : 2 * BLOCKS, :] = pltpu.roll(piece, PART * s, 1) if s else piece
     for f in range(SUBS):
         for a in range(TILES):
+            if f == 0 and a == 0:
+                continue
             tile = None
             for v in range(SUBS):
                 b = 2 * a - 1 - v
@@ -93,6 +95,8 @@
         left = []
         for f in range(SUBS):
             for a in range(TILES):
+                if f == 0 and a == 0:
+                    continue
                 left.append(
                     jnp.concatenate(
                         [
@@ -119,7 +123,7 @@
     lane = lax.broadcasted_iota(jnp.int32, (BLOCKS, LANES), 1)
     for a in range(TILES - 1):
         for f in range(SUBS):
-            row = BLOCKS * (TILES * f + a + 1)
+            row = BLOCKS * (TILES * f + a)
             first = total[row : row + BLOCKS, 0:LANES]
             second = total[row : row + BLOCKS, LANES : 2 * LANES]
             if f == 0:
@@ -140,7 +144,7 @@
     stage, packed, got, w_got,
     taps, wide, x_own, g_own, mixed, masks, turned, base0, edges0, total0, base1, edges1, total1,
     ready, back, regroup, sliced, part, result,
-    load_sem, own_sem, in_send, in_recv, w_send, w_recv,
+    w_wide, w_sorted, load_sem, own_sem, in_send, in_recv, w_send, w_recv,
     m_send, m_recv, t_send, t_recv, o_send, o_recv,
 ):
     me_c, me_h = lax.axis_index("ctx"), lax.axis_index("head")
@@ -153,7 +157,7 @@
         )
 
     def w_copy(k):
-        return remote(w_in, w_got.at[me_h], w_send.at[k], w_recv.at[k], "head", k)
+        return remote(w_sorted, w_got.at[me_h], w_send.at[k], w_recv.at[k], "head", k)
 
     def in_copy(leg, k):
         rows = pl.ds(*LEGS[leg])
@@ -169,9 +173,11 @@
             ready.at[peer, rows], back.at[me_c, rows], m_send.at[t, k], m_recv.at[t, k], "ctx", k
         )
 
-    def t_copy(k):
+    def t_copy(t, k):
         peer = lax.rem(me_h + k, NH)
-        return remote(sliced.at[peer], part.at[me_h], t_send.at[k], t_recv.at[k], "head", k)
+        return remote(
+            sliced.at[t, peer], part.at[t, me_h], t_send.at[t, k], t_recv.at[t, k], "head", k
+        )
 
     columns = pl.ds(pl.multiple_of(me_h * LANES, LANES), LANES)
 
@@ -232,13 +238,20 @@
     for m in range(MINE):
         pack(2, m)
     depart(2)
+    for j in range(4):
+        w_wide[j] = w_in[:, LANES * j : LANES * (j + 1)].astype(F32)
+        for m in range(0, MINE, 2):
+            rows = [w_wide[j, pl.ds(m + i, NC, stride=MINE), :] for i in range(2)]
+            w_sorted[NC * m : NC * (m + 2), LANES * j : LANES * (j + 1)] = jnp.concatenate(
+                rows, axis=0
+            ).astype(BF16)
     for k in range(1, NH):
         w_copy(k).start()
     own = [
         pltpu.make_async_copy(a, b, own_sem.at[i])
         for i, (a, b) in enumerate(
             (
-                (packed.at[me_c], got.at[me_c]), (w_in, w_got.at[me_h]),
+                (packed.at[me_c], got.at[me_c]), (w_sorted, w_got.at[me_h]),
             )
         )
     ]
@@ -302,25 +315,37 @@
     for t in range(2):
         for k in range(1, NC):
             m_copy(t, k).wait()
-    for c in range(NC):
-        stage[0, 64 * c : 64 * c + 64, :] = jnp.where(
-            me_c == c, ready[c].astype(F32), back[c].astype(F32)
-        )
-    for t in range(NH):
-        sliced[t] = stage[0, pl.ds(t, CH, stride=NH), :].astype(BF16)
-    for k in range(1, NH):
-        t_copy(k).start()
-    copy = pltpu.make_async_copy(sliced.at[me_h], part.at[me_h], own_sem.at[3])
-    copy.start()
-    copy.wait()
+        for c in range(NC):
+            rows = slice(2 * ROWS * t, 2 * ROWS * (t + 1))
+            stage[t, 2 * ROWS * c : 2 * ROWS * (c + 1), :] = jnp.where(
+                me_c == c, ready[c, rows, :].astype(F32), back[c, rows, :].astype(F32)
+            )
+        for h in range(NH):
+            rows = [stage[t, pl.ds(ROWS * i + h, NC, stride=2 * ROWS), :] for i in range(2)]
+            sliced[t, h] = jnp.concatenate(rows, axis=0).astype(BF16)
+        for k in range(1, NH):
+            t_copy(t, k).start()
+    own = [
+        pltpu.make_async_copy(sliced.at[t, me_h], part.at[t, me_h], own_sem.at[3 + t])
+        for t in range(2)
+    ]
+    for copy in own:
+        copy.start()
+    for copy in own:
+        copy.wait()
     for k in range(1, NH):
         w_copy(k).wait()
-    for k in range(1, NH):
-        t_copy(k).wait()
-    total = lax.dot_general(
-        w_got[...].reshape(NH * CH, NH * CH), part[...].reshape(NH * CH, LANES),
-        (((0,), (0,)), ((), ())), preferred_element_type=F32,
-    )
+    total = None
+    for t in range(2):
+        for k in range(1, NH):
+            t_copy(t, k).wait()
+        half = lax.dot_general(
+            w_got[:, 16 * t : 16 * t + 16, :].reshape(NH * 16, NH * CH),
+            part[t].reshape(NH * 16, LANES),
+            (((0,), (0,)), ((), ())),
+            preferred_element_type=F32,
+        )
+        total = half if t == 0 else total + half
     for t in range(NH):
         result[t] = total[CH * t : CH * (t + 1), :]
     for k in range(1, NH):
@@ -355,17 +380,19 @@
             *[
                 vmem((SUBS, TILES, 2 * BLOCKS, LANES), F32),
                 vmem((PART * (PIECES + 1), LANES), BF16),
-                vmem((SUBS * TILES * BLOCKS, 2 * LANES), F32),
+                vmem(((SUBS * TILES - 1) * BLOCKS, 2 * LANES), F32),
             ]
             * 2,
             vmem((NC, MINE * ROWS, LANES), BF16),
             vmem((NC, MINE * ROWS, LANES), BF16),
             vmem((NC * 8, LANES), F32),
-            vmem((NH, CH, LANES), BF16),
-            vmem((NH, CH, LANES), BF16),
+            vmem((2, NH, 16, LANES), BF16),
+            vmem((2, NH, 16, LANES), BF16),
             vmem((NH, CH, LANES), F32),
+            vmem((4, CH, LANES), F32),
+            vmem((CH, NH * CH), BF16),
             dma((6,)), dma((6,)), dma((3, NC)), dma((3, NC)), dma((NH,)), dma((NH,)),
-            dma((2, NC)), dma((2, NC)), dma((NH,)), dma((NH,)), dma((NH,)), dma((NH,)),
+            dma((2, NC)), dma((2, NC)), dma((2, NH)), dma((2, NH)), dma((NH,)), dma((NH,)),
         ],
         compiler_params=pltpu.CompilerParams(
             collective_id=0, has_side_effects=True, vmem_limit_bytes=40 << 20

time: 35 us -> 34.9 us (level)
  no operation moved by 1% of the time
where the time goes in v6:
time: 34.9 us; the launch traced here: 34.8 us
  Pallas kernels  34.1 us (98%)
  local copies, waits for them, and re-layouts  0.71 us (2%)
    pallas_call x1, Pallas kernels, local(): pl.pallas_call(kernel, out_shape=jax.ShapeDtypeStruct((CH, NH * LANES), F...  34.1 us
    unnamed x1, local copies, waits for them, and re-layouts  0.71 us

profile of v6, /device:TPU:0, one launch (start us, length us, event | category | flops | bytes accessed | tf_op | source)
XLA Modules:
  0.0 34.8 jit_solution(8959686883971328308)
XLA Ops:
  0.0 34.1 %shard_map.64 = f32[32,2048]{1,0:T(8,128)S(1)} custom-call(bf16[32,2048]{1,0:T(8,128)(2,1)} %x_hbm.1, bf16[32,2048]{1,0:T(8,128)(2,1)} %g_hbm.1, f32[32,2048]{1,0:T(8,128)} %h_hbm.1, bf16[32,512]{1,0:T(8,128)(2,1)} %w_hbm.1, s32[2,4]{1,0:T(2,128)} %far_hbm.1, f32[32]{0:T(128)} %skip_hbm.1), custom_call_target="tpu_custom_call" | custom-call | tf_op jit(solution)/shard_map/pallas_call | solution.py:365
  34.1 0.7 %copy.8 = f32[32,2048]{1,0:T(8,128)} copy(f32[32,2048]{1,0:T(8,128)S(1)} %shard_map.64) | data formatting | bytes 524288

commit v7 on v5

--- a/solution.py
+++ b/solution.py
@@ -72,6 +72,8 @@
             turned[b, s, BLOCKS : 2 * BLOCKS, :] = pltpu.roll(piece, PART * s, 1) if s else piece
     for f in range(SUBS):
         for a in range(TILES):
+            if f == 0 and a == 0:
+                continue
             tile = None
             for v in range(SUBS):
                 b = 2 * a - 1 - v
@@ -93,6 +95,8 @@
         left = []
         for f in range(SUBS):
             for a in range(TILES):
+                if f == 0 and a == 0:
+                    continue
                 left.append(
                     jnp.concatenate(
                         [
@@ -119,7 +123,7 @@
     lane = lax.broadcasted_iota(jnp.int32, (BLOCKS, LANES), 1)
     for a in range(TILES - 1):
         for f in range(SUBS):
-            row = BLOCKS * (TILES * f + a + 1)
+            row = BLOCKS * (TILES * f + a)
             first = total[row : row + BLOCKS, 0:LANES]
             second = total[row : row + BLOCKS, LANES : 2 * LANES]
             if f == 0:
@@ -355,7 +359,7 @@
             *[
                 vmem((SUBS, TILES, 2 * BLOCKS, LANES), F32),
                 vmem((PART * (PIECES + 1), LANES), BF16),
-                vmem((SUBS * TILES * BLOCKS, 2 * LANES), F32),
+                vmem(((SUBS * TILES - 1) * BLOCKS, 2 * LANES), F32),
             ]
             * 2,
             vmem((NC, MINE * ROWS, LANES), BF16),

time: 35 us -> 35 us (level)
  no operation moved by 1% of the time
where the time goes in v7:
time: 35 us; the launch traced here: 34.9 us
  Pallas kernels  34.2 us (98%)
  local copies, waits for them, and re-layouts  0.71 us (2%)
    pallas_call x1, Pallas kernels, local(): pl.pallas_call(kernel, out_shape=jax.ShapeDtypeStruct((CH, NH * LANES), F...  34.2 us
    unnamed x1, local copies, waits for them, and re-layouts  0.71 us

profile of v7, /device:TPU:0, one launch (start us, length us, event | category | flops | bytes accessed | tf_op | source)
XLA Modules:
  0.0 34.9 jit_solution(449654724432647678)
XLA Ops:
  0.0 34.2 %shard_map.64 = f32[32,2048]{1,0:T(8,128)S(1)} custom-call(bf16[32,2048]{1,0:T(8,128)(2,1)} %x_hbm.1, bf16[32,2048]{1,0:T(8,128)(2,1)} %g_hbm.1, f32[32,2048]{1,0:T(8,128)} %h_hbm.1, bf16[32,512]{1,0:T(8,128)(2,1)} %w_hbm.1, s32[2,4]{1,0:T(2,128)} %far_hbm.1, f32[32]{0:T(128)} %skip_hbm.1), custom_call_target="tpu_custom_call" | custom-call | tf_op jit(solution)/shard_map/pallas_call | solution.py:344
  34.2 0.7 %copy.8 = f32[32,2048]{1,0:T(8,128)} copy(f32[32,2048]{1,0:T(8,128)S(1)} %shard_map.64) | data formatting | bytes 524288
